TPU v7x, 512 devices: a whole 4x4x16 slice. The times are simulated.
512 devices in a mesh: dp: 2 (over x_hi), row: 16 (over z), col: 16 (over y, x_lo, core).
Axes of the slice: x: 4 (x_hi: 2, x_lo: 2; x = x_hi * 2 + x_lo), y: 4, z: 16, core: 2. Of those that a mesh axis runs over, the one named last changes fastest.
Arguments:
- gate_query: bfloat16 [2, 16, 512, 2048], P('dp', None, 'row', 'col'), may hold values from -6 to 6
- gate_key: bfloat16 [2, 16, 512, 2048], P('dp', None, 'row', 'col'), may hold values from -6 to 6
- value_input: bfloat16 [2, 16, 512, 2048], P('dp', None, 'row', 'col'), may hold values from -6 to 6
- grad_output: bfloat16 [2, 16, 512, 2048], P('dp', None, 'row', 'col'), may hold values from -6 to 6
- filter_spec: bfloat16 [2, 16, 1024, 2048], P(None, 'row', 'col'), may hold values from -6 to 6
- skip_gain: float32 [16], replicated, may hold values from 0.5 to 2
Outputs:
- grad_query: bfloat16 [2, 16, 512, 2048], P('dp', None, 'row', 'col')
- grad_key: bfloat16 [2, 16, 512, 2048], P('dp', None, 'row', 'col')
- grad_value: bfloat16 [2, 16, 512, 2048], P('dp', None, 'row', 'col')
- filter_grad: bfloat16 [2, 16, 1024, 2048], P(None, 'row', 'col')
All inputs are finite; a program needn't handle non-finite values.
Results may differ from a plain program's by a relative error of at most 0.0057.
Values may be sent and summed in bfloat16 or wider, within the bound.
A program may use at most 64 MiB of HBM per device.

v0:
```python
import math

import jax
import jax.numpy as jnp
from jax import lax
from jax.sharding import PartitionSpec as P


def global_phase(row_count, col_count, row_start, col_start, period, direction):
    row_index = lax.broadcasted_iota(jnp.int32, (row_count, col_count), 0) + row_start
    col_index = lax.broadcasted_iota(jnp.int32, (row_count, col_count), 1) + col_start
    angles = 2.0 * math.pi / period * (row_index * col_index % period).astype(jnp.float32)
    return (jnp.cos(angles), direction * jnp.sin(angles))


def rotate(real_part, imag_part, cos_part, sin_part):
    return (
        real_part * cos_part - imag_part * sin_part,
        real_part * sin_part + imag_part * cos_part,
    )


def contract(left_form, table_form, out_form, real_part, imag_part, cos_part, sin_part):
    stacked = jnp.stack([real_part, imag_part])
    table = jnp.stack([jnp.stack([cos_part, -sin_part]), jnp.stack([sin_part, cos_part])])
    result = jnp.einsum(
        "i" + left_form + ",oi" + table_form + "->o" + out_form,
        stacked,
        table,
        precision=lax.Precision.HIGHEST,
    )
    return (result[0], result[1])


def forward_rows(signal, col_start, total_len):
    sequences, channels, half_rows, col_count = signal.shape
    length = 2 * half_rows
    inner_size = min(128, length)
    outer_size = length // inner_size
    half_inner = inner_size // 2
    highest = lax.Precision.HIGHEST
    values = signal.astype(jnp.float32).reshape(
        sequences * channels, half_inner, outer_size, col_count
    )
    cos_inner, sin_inner = global_phase(inner_size, half_inner, 0, 0, inner_size, -1.0)
    real_part = jnp.einsum("sbaj,kb->skaj", values, cos_inner, precision=highest)
    imag_part = jnp.einsum("sbaj,kb->skaj", values, sin_inner, precision=highest)
    cos_twist, sin_twist = global_phase(inner_size, outer_size, 0, 0, length, -1.0)
    real_part, imag_part = rotate(
        real_part, imag_part, cos_twist[None, :, :, None], sin_twist[None, :, :, None]
    )
    cos_outer, sin_outer = global_phase(outer_size, outer_size, 0, 0, outer_size, -1.0)
    real_part, imag_part = contract(
        "skaj", "ma", "smkj", real_part, imag_part, cos_outer, sin_outer
    )
    real_part = real_part.reshape(sequences * channels, length, col_count)
    imag_part = imag_part.reshape(sequences * channels, length, col_count)
    cos_global, sin_global = global_phase(length, col_count, 0, col_start, total_len, -1.0)
    real_part, imag_part = rotate(real_part, imag_part, cos_global[None], sin_global[None])
    return (
        real_part.reshape(sequences, channels, length, col_count),
        imag_part.reshape(sequences, channels, length, col_count),
    )


def forward_cols(real_part, imag_part):
    sequences, channels, row_count, length = real_part.shape
    inner_size = min(128, length)
    outer_size = length // inner_size
    grid_shape = (sequences * channels, row_count, outer_size, inner_size)
    real_part = real_part.reshape(grid_shape)
    imag_part = imag_part.reshape(grid_shape)
    cos_outer, sin_outer = global_phase(outer_size, outer_size, 0, 0, outer_size, -1.0)
    real_part, imag_part = contract(
        "srab", "ma", "srmb", real_part, imag_part, cos_outer, sin_outer
    )
    cos_twist, sin_twist = global_phase(outer_size, inner_size, 0, 0, length, -1.0)
    real_part, imag_part = rotate(real_part, imag_part, cos_twist, sin_twist)
    cos_inner, sin_inner = global_phase(inner_size, inner_size, 0, 0, inner_size, -1.0)
    real_part, imag_part = contract(
        "srmb", "kb", "srmk", real_part, imag_part, cos_inner, sin_inner
    )
    return (
        real_part.reshape(sequences, channels, row_count, length),
        imag_part.reshape(sequences, channels, row_count, length),
    )


def inverse_cols(real_part, imag_part, row_start, total_len):
    sequences, channels, row_count, length = real_part.shape
    inner_size = min(128, length)
    outer_size = length // inner_size
    grid_shape = (sequences * channels, row_count, outer_size, inner_size)
    real_part = real_part.reshape(grid_shape)
    imag_part = imag_part.reshape(grid_shape)
    cos_inner, sin_inner = global_phase(inner_size, inner_size, 0, 0, inner_size, 1.0)
    real_part, imag_part = contract(
        "srmk", "bk", "srmb", real_part, imag_part, cos_inner, sin_inner
    )
    cos_twist, sin_twist = global_phase(outer_size, inner_size, 0, 0, length, 1.0)
    real_part, imag_part = rotate(real_part, imag_part, cos_twist, sin_twist)
    cos_outer, sin_outer = global_phase(outer_size, outer_size, 0, 0, outer_size, 1.0)
    real_part, imag_part = contract(
        "srmb", "am", "srab", real_part, imag_part, cos_outer, sin_outer
    )
    real_part = real_part.reshape(sequences * channels, row_count, length)
    imag_part = imag_part.reshape(sequences * channels, row_count, length)
    cos_global, sin_global = global_phase(row_count, length, row_start, 0, total_len, 1.0)
    real_part, imag_part = rotate(real_part, imag_part, cos_global[None], sin_global[None])
    return (
        real_part.reshape(sequences, channels, row_count, length),
        imag_part.reshape(sequences, channels, row_count, length),
    )


def inverse_rows(real_part, imag_part, total_len):
    sequences, channels, length, col_count = real_part.shape
    inner_size = min(128, length)
    outer_size = length // inner_size
    half_inner = inner_size // 2
    highest = lax.Precision.HIGHEST
    grid_shape = (sequences * channels, outer_size, inner_size, col_count)
    real_part = real_part.reshape(grid_shape)
    imag_part = imag_part.reshape(grid_shape)
    cos_outer, sin_outer = global_phase(outer_size, outer_size, 0, 0, outer_size, 1.0)
    real_part, imag_part = contract(
        "smkj", "am", "sakj", real_part, imag_part, cos_outer, sin_outer
    )
    cos_twist, sin_twist = global_phase(outer_size, inner_size, 0, 0, length, 1.0)
    real_part, imag_part = rotate(
        real_part, imag_part, cos_twist[None, :, :, None], sin_twist[None, :, :, None]
    )
    cos_inner, sin_inner = global_phase(half_inner, inner_size, 0, 0, inner_size, 1.0)
    stacked = jnp.stack([real_part, imag_part])
    table = jnp.stack([cos_inner, -sin_inner])
    result = jnp.einsum("isakj,ibk->sbaj", stacked, table, precision=highest)
    result = result * (1.0 / total_len)
    return result.reshape(sequences, channels, half_inner * outer_size, col_count)


def to_internal(spec_plane):
    channels, row_count, length = spec_plane.shape
    inner_size = min(128, length)
    outer_size = length // inner_size
    grid = spec_plane.astype(jnp.float32).reshape(channels, row_count, inner_size, outer_size)
    return jnp.swapaxes(grid, 2, 3).reshape(1, channels, row_count, length)


def from_internal(spec_plane):
    sequences, channels, row_count, length = spec_plane.shape
    inner_size = min(128, length)
    outer_size = length // inner_size
    grid = spec_plane.reshape(channels, row_count, outer_size, inner_size)
    return jnp.swapaxes(grid, 2, 3).reshape(channels, row_count, length)


def shards(gate_query, gate_key, value_input, grad_output, filter_spec, skip_gain):
    mixed = (gate_key.astype(jnp.float32) * value_input.astype(jnp.float32)).astype(jnp.bfloat16)
    gated = (grad_output.astype(jnp.float32) * gate_query.astype(jnp.float32)).astype(jnp.bfloat16)
    col_place = lax.axis_index("col")
    col_count = gate_query.shape[3]
    row_len = 2 * gate_query.shape[2] * lax.axis_size("row")
    col_len = col_count * lax.axis_size("col")
    total_len = row_len * col_len
    col_start = col_place * col_count
    freq_rows = row_len // lax.axis_size("col")
    freq_start = col_place * freq_rows
    spec_real = to_internal(filter_spec[0])
    spec_imag = to_internal(filter_spec[1])
    inverse_n = 1.0 / total_len
    mixed_cols, gated_cols = (
        lax.all_to_all(mixed, "row", split_axis=1, concat_axis=2, tiled=True),
        lax.all_to_all(gated, "row", split_axis=1, concat_axis=2, tiled=True),
    )
    mixed_re, mixed_im = forward_rows(mixed_cols, col_start, total_len)
    gated_re, gated_im = forward_rows(gated_cols, col_start, total_len)
    pieces = (
        lax.all_to_all(mixed_re, "col", split_axis=2, concat_axis=3, tiled=True),
        lax.all_to_all(mixed_im, "col", split_axis=2, concat_axis=3, tiled=True),
        lax.all_to_all(gated_re, "col", split_axis=2, concat_axis=3, tiled=True),
        lax.all_to_all(gated_im, "col", split_axis=2, concat_axis=3, tiled=True),
    )
    first_pair = forward_cols(pieces[0], pieces[1])
    second_pair = forward_cols(pieces[2], pieces[3])
    mixed_re = first_pair[0]
    mixed_im = first_pair[1]
    gated_re = second_pair[0]
    gated_im = second_pair[1]
    conv_re, conv_im = inverse_cols(
        spec_real * mixed_re - spec_imag * mixed_im,
        spec_real * mixed_im + spec_imag * mixed_re,
        freq_start,
        total_len,
    )
    corr_re, corr_im = inverse_cols(
        spec_real * gated_re + spec_imag * gated_im,
        spec_real * gated_im - spec_imag * gated_re,
        freq_start,
        total_len,
    )
    pieces = (
        lax.all_to_all(conv_re, "col", split_axis=3, concat_axis=2, tiled=True),
        lax.all_to_all(conv_im, "col", split_axis=3, concat_axis=2, tiled=True),
        lax.all_to_all(corr_re, "col", split_axis=3, concat_axis=2, tiled=True),
        lax.all_to_all(corr_im, "col", split_axis=3, concat_axis=2, tiled=True),
    )
    conv_rows = inverse_rows(pieces[0], pieces[1], total_len)
    corr_rows = inverse_rows(pieces[2], pieces[3], total_len)
    convolved, correlated = (
        lax.all_to_all(conv_rows, "row", split_axis=2, concat_axis=1, tiled=True),
        lax.all_to_all(corr_rows, "row", split_axis=2, concat_axis=1, tiled=True),
    )
    grad_real = (mixed_re * gated_re + mixed_im * gated_im) * inverse_n
    grad_imag = (mixed_re * gated_im - mixed_im * gated_re) * inverse_n
    grad_real, grad_imag = lax.psum((grad_real, grad_imag), "dp")
    filter_grad = jnp.stack([from_internal(grad_real), from_internal(grad_imag)]).astype(
        jnp.bfloat16
    )
    gain_wide = skip_gain[None, :, None, None]
    grad_query = (
        grad_output.astype(jnp.float32) * (convolved + gain_wide * mixed.astype(jnp.float32))
    ).astype(jnp.bfloat16)
    grad_mixed = correlated + gain_wide * gated.astype(jnp.float32)
    grad_key = (grad_mixed * value_input.astype(jnp.float32)).astype(jnp.bfloat16)
    grad_value = (grad_mixed * gate_key.astype(jnp.float32)).astype(jnp.bfloat16)
    return (grad_query, grad_key, grad_value, filter_grad)


def solution(mesh):
    in_specs = (
        P("dp", None, "row", "col"),
        P("dp", None, "row", "col"),
        P("dp", None, "row", "col"),
        P("dp", None, "row", "col"),
        P(None, "row", "col", None),
        P(),
    )
    out_specs = (
        P("dp", None, "row", "col"),
        P("dp", None, "row", "col"),
        P("dp", None, "row", "col"),
        P(None, "row", "col", None),
    )
    return jax.shard_map(shards, mesh=mesh, in_specs=in_specs, out_specs=out_specs, check_vma=False)
```

profile of v0, /device:TPU:32, one launch (start us, length us, event | category | flops | bytes accessed | tf_op | source)
XLA Modules:
  0.0 472.3 jit_solution(16132769396655485070)
XLA Ops:
  0.6 1.7 fusion.47
  2.3 15.3 %all-to-all-start.6 = ((bf16[1,16,32,128]{3,2,0,1:T(8,128)(2,1)}), bf16[1,16,32,128]{3,2,0,1:T(8,128)(2,1)S(1)}, u32[]{:S(2)}, u32[]{:S(2)}) async-start(bf16[1,16,32,128]{3,2,0,1:T(8,128)(2,1)} %fusion.47), calls=%async_computation.6 | async-start | bytes 262144 | tf_op jit(solution)/shard_map/all_to_all | solution.py:173
  19.2 12.6 %all-to-all-done.6 = bf16[1,16,32,128]{3,2,0,1:T(8,128)(2,1)S(1)} async-done(((bf16[1,16,32,128]{3,2,0,1:T(8,128)(2,1)}), bf16[1,16,32,128]{3,2,0,1:T(8,128)(2,1)S(1)}, u32[]{:S(2)}, u32[]{:S(2)}) %all-to-all-start.6) | async-done | bytes 131104 | tf_op jit(solution)/shard_map/all_to_all | solution.py:173
  31.9 4.3 all-to-all-start
  37.3 12.3 %all-to-all-done = bf16[1,16,32,128]{3,2,0,1:T(8,128)(2,1)S(1)} async-done(((bf16[1,16,32,128]{3,2,0,1:T(8,128)(2,1)}), bf16[1,16,32,128]{3,2,0,1:T(8,128)(2,1)S(1)}, u32[]{:S(2)}, u32[]{:S(2)}) %all-to-all-start) | async-done | bytes 131104 | tf_op jit(solution)/shard_map/all_to_all | solution.py:172
  51.2 1.5 convolution_bitcast_fusion.5
  53.0 1.5 convolution_bitcast_fusion.11
  54.8 3.2 fusion.32
  58.1 16.2 %all_to_all.162 = f32[1,1,1024,128]{3,1,0,2:T(1,128)S(1)} all-to-all(f32[1,1,1024,128]{3,1,0,2:T(1,128)S(1)} %bitcast.403), channel_id=1, replica_groups=mesh['dp'=2,'row'=16,'col'=16] {'col'}, dimensions={2} | all-to-all | bytes 1048576 | tf_op jit(solution)/shard_map/all_to_all | solution.py:181
  74.2 3.6 all-to-all-start.7
  79.6 9.1 %all-to-all-done.7 = f32[1,1,1024,128]{3,1,0,2:T(1,128)S(1)} async-done(((f32[1,1,1024,128]{3,1,0,2:T(1,128)}), f32[1,1,1024,128]{3,1,0,2:T(1,128)S(1)}, u32[]{:S(2)}, u32[]{:S(2)}) %all-to-all-start.7) | async-done | bytes 524320 | tf_op jit(solution)/shard_map/all_to_all | solution.py:180
  88.6 3.7 all-to-all-start.2
  93.1 10.1 %all-to-all-done.2 = f32[1,1,1024,128]{3,1,0,2:T(1,128)S(1)} async-done(((f32[1,1,1024,128]{3,1,0,2:T(1,128)}), f32[1,1,1024,128]{3,1,0,2:T(1,128)S(1)}, u32[]{:S(2)}, u32[]{:S(2)}) %all-to-all-start.2) | async-done | bytes 524320 | tf_op jit(solution)/shard_map/all_to_all | solution.py:179
  104.0 4.5 all-to-all-start.1
  114.8 4.3 all-to-all-done.1
  119.1 1.4 copy.393
  124.3 1.2 convolution_bitcast_fusion.9
  125.6 1.4 add_multiply_fusion
  128.0 1.6 convolution_bitcast_fusion.2
  129.6 1.6 convolution_bitcast_fusion.8
  135.4 4.5 multiply_subtract_fusion
  141.0 9.3 %reduce.4 = f32[2048,64]{1,0:T(8,128)S(1)} reduce(f32[2048,1,1,64]{3,2,1,0:T(1,128)S(1)} %bitcast.389, f32[]{:T(128)} %broadcast.1577), dimensions={1,2}, to_apply=%bitcast.371.reduce_sub_computation | reduce | bytes 1048580
  150.3 1.5 reshape.1451
  151.8 4.6 all-to-all-start.10
  157.0 9.3 %reduce.6 = f32[2048,64]{1,0:T(8,128)S(1)} reduce(f32[2048,1,1,64]{3,2,1,0:T(1,128)S(1)} %bitcast.390, f32[]{:T(128)} %broadcast.1577), dimensions={1,2}, to_apply=%bitcast.373.reduce_sub_computation | reduce | bytes 1048580
  166.3 1.5 reshape.1453
  167.8 5.8 %all-to-all-start.9 = ((f32[16,1,8192]{2,1,0:T(1,128)}), f32[16,1,8192]{2,1,0:T(1,128)}, u32[]{:S(2)}, u32[]{:S(2)}) async-start(f32[16,1,8192]{2,1,0:T(1,128)} %reshape.1453), calls=%async_computation.9 | async-start | bytes 1048576 | tf_op jit(solution)/shard_map/all_to_all | solution.py:204
  174.2 9.3 %reduce.8 = f32[2048,64]{1,0:T(8,128)S(1)} reduce(f32[2048,1,1,64]{3,2,1,0:T(1,128)S(1)} %bitcast.391, f32[]{:T(128)} %broadcast.1577), dimensions={1,2}, to_apply=%bitcast.367.reduce_sub_computation | reduce | bytes 1048580
  183.5 1.5 reshape.1447
  185.0 5.9 %all-to-all-start.4 = ((f32[16,1,8192]{2,1,0:T(1,128)}), f32[16,1,8192]{2,1,0:T(1,128)S(1)}, u32[]{:S(2)}, u32[]{:S(2)}) async-start(f32[16,1,8192]{2,1,0:T(1,128)} %reshape.1447), calls=%async_computation.4 | async-start | bytes 1048576 | tf_op jit(solution)/shard_map/all_to_all | solution.py:203
  191.5 9.3 %reduce.10 = f32[2048,64]{1,0:T(8,128)S(1)} reduce(f32[2048,1,1,64]{3,2,1,0:T(1,128)S(1)} %bitcast.392, f32[]{:T(128)} %broadcast.1577), dimensions={1,2}, to_apply=%bitcast.369.reduce_sub_computation | reduce | bytes 1048580
  200.8 1.5 reshape.1449
  202.3 5.8 %all-to-all-start.3 = ((f32[16,1,8192]{2,1,0:T(1,128)}), f32[16,1,8192]{2,1,0:T(1,128)S(1)}, u32[]{:S(2)}, u32[]{:S(2)}) async-start(f32[16,1,8192]{2,1,0:T(1,128)} %reshape.1449), calls=%async_computation.3 | async-start | bytes 1048576 | tf_op jit(solution)/shard_map/all_to_all | solution.py:202
  208.6 3.0 reduce.5
  211.6 1.3 reshape.1452
  214.9 2.9 reduce.7
  217.8 1.3 reshape.1454
  221.1 1.9 reduce.9
  223.0 1.3 reshape.1448
  225.9 1.9 reduce.11
  227.8 1.3 reshape.1450
  235.5 4.5 all-to-all-start.11
  241.4 196.4 %all-reduce.2 = (bf16[1,1,64,2048]{3,1,2,0:T(2,128)(2,1)}, bf16[1,1,64,2048]{3,1,2,0:T(2,128)(2,1)S(1)}) all-reduce(f32[1,1,64,2048]{3,1,2,0:T(1,128)S(1)} %bitcast.411, f32[1,1,64,2048]{3,1,2,0:T(1,128)S(1)} %bitcast.412), channel_id=1, replica_groups=mesh['dp'=2,'row'=16,'col'=16] {'dp'}, use_global_device_ids=true, to_apply=%region_1.2 | all-reduce | flops 262144 | bytes 1572864 | tf_op jit(solution)/shard_map/psum | solution.py:215
  439.6 12.3 %all-to-all-start.5 = ((f32[1,1,512,128]{3,1,0,2:T(1,128)}), f32[1,1,512,128]{3,1,0,2:T(1,128)S(1)}, u32[]{:S(2)}, u32[]{:S(2)}) async-start(f32[1,1,512,128]{3,1,0,2:T(1,128)} %bitcast.96), calls=%async_computation.5 | async-start | bytes 524288 | tf_op jit(solution)/shard_map/all_to_all | solution.py:210
  451.9 1.4 convert_reduce_fusion
  454.0 1.4 convert_reduce_fusion.1
  457.5 12.1 %all-to-all-done.5 = f32[1,1,512,128]{3,1,0,2:T(1,128)S(1)} async-done(((f32[1,1,512,128]{3,1,0,2:T(1,128)}), f32[1,1,512,128]{3,1,0,2:T(1,128)S(1)}, u32[]{:S(2)}, u32[]{:S(2)}) %all-to-all-start.5) | async-done | bytes 262176 | tf_op jit(solution)/shard_map/all_to_all | solution.py:210
  470.2 1.9 fusion.59
  (155 shorter events, 44.6 us)
Async XLA Ops:
  2.3 16.2 %copy-start.11 = (bf16[1,16,32,128]{3,2,1,0:T(8,128)(2,1)S(1)}, bf16[1,16,32,128]{3,2,1,0:T(8,128)(2,1)}, u32[]{:S(2)}) copy-start(bf16[1,16,32,128]{3,2,1,0:T(8,128)(2,1)} %param.8) | copy-start | bytes 393220
  2.3 16.2 %copy-start.13 = (bf16[1,16,32,128]{3,2,1,0:T(8,128)(2,1)S(1)}, bf16[1,16,32,128]{3,2,1,0:T(8,128)(2,1)}, u32[]{:S(2)}) copy-start(bf16[1,16,32,128]{3,2,1,0:T(8,128)(2,1)} %param.7) | copy-start | bytes 393220
  2.3 29.6 %all-to-all-start.6 = ((bf16[1,16,32,128]{3,2,0,1:T(8,128)(2,1)}), bf16[1,16,32,128]{3,2,0,1:T(8,128)(2,1)S(1)}, u32[]{:S(2)}, u32[]{:S(2)}) async-start(bf16[1,16,32,128]{3,2,0,1:T(8,128)(2,1)} %fusion.47), calls=%async_computation.6 | async-start | bytes 262144 | tf_op jit(solution)/shard_map/all_to_all | solution.py:173
  31.9 17.8 %all-to-all-start = ((bf16[1,16,32,128]{3,2,0,1:T(8,128)(2,1)}), bf16[1,16,32,128]{3,2,0,1:T(8,128)(2,1)S(1)}, u32[]{:S(2)}, u32[]{:S(2)}) async-start(bf16[1,16,32,128]{3,2,0,1:T(8,128)(2,1)} %fusion.49), calls=%async_computation | async-start | bytes 262144 | tf_op jit(solution)/shard_map/all_to_all | solution.py:172
  74.2 14.4 %all-to-all-start.7 = ((f32[1,1,1024,128]{3,1,0,2:T(1,128)}), f32[1,1,1024,128]{3,1,0,2:T(1,128)S(1)}, u32[]{:S(2)}, u32[]{:S(2)}) async-start(f32[1,1,1024,128]{3,1,0,2:T(1,128)} %bitcast.115), calls=%async_computation.7 | async-start | bytes 1048576 | tf_op jit(solution)/shard_map/all_to_all | solution.py:180
  88.6 4.4 copy-start.9
  88.6 14.5 %all-to-all-start.2 = ((f32[1,1,1024,128]{3,1,0,2:T(1,128)}), f32[1,1,1024,128]{3,1,0,2:T(1,128)S(1)}, u32[]{:S(2)}, u32[]{:S(2)}) async-start(f32[1,1,1024,128]{3,1,0,2:T(1,128)} %bitcast.45), calls=%async_computation.2 | async-start | bytes 1048576 | tf_op jit(solution)/shard_map/all_to_all | solution.py:179
  103.2 0.8 copy-start.3
  104.0 15.1 %all-to-all-start.1 = ((f32[1,1,1024,128]{3,1,0,2:T(1,128)}), f32[1,1,1024,128]{3,1,0,2:T(1,128)}, u32[]{:S(2)}, u32[]{:S(2)}) async-start(f32[1,1,1024,128]{3,1,0,2:T(1,128)} %bitcast.42), calls=%async_computation.1 | async-start | bytes 1048576 | tf_op jit(solution)/shard_map/all_to_all | solution.py:178
  111.5 0.8 copy-start.16
  113.3 1.1 copy-start.4
  119.1 1.4 copy-start.7
  119.1 1.4 copy-start.18
  119.1 1.4 copy-start.19
  121.6 1.1 copy-start.20
  121.6 1.1 copy-start.24
  127.1 0.9 copy-start.8
  129.6 1.6 copy-start.23
  131.2 0.8 copy-start.17
  134.5 0.9 copy-start.26
  151.8 4.6 copy-start
  151.8 16.0 %all-to-all-start.10 = ((f32[16,1,8192]{2,1,0:T(1,128)}), f32[16,1,8192]{2,1,0:T(1,128)}, u32[]{:S(2)}, u32[]{:S(2)}) async-start(f32[16,1,8192]{2,1,0:T(1,128)} %reshape.1451), calls=%async_computation.10 | async-start | bytes 1048576 | tf_op jit(solution)/shard_map/all_to_all | solution.py:205
  167.8 17.2 %all-to-all-start.9 = ((f32[16,1,8192]{2,1,0:T(1,128)}), f32[16,1,8192]{2,1,0:T(1,128)}, u32[]{:S(2)}, u32[]{:S(2)}) async-start(f32[16,1,8192]{2,1,0:T(1,128)} %reshape.1453), calls=%async_computation.9 | async-start | bytes 1048576 | tf_op jit(solution)/shard_map/all_to_all | solution.py:204
  185.0 17.3 %all-to-all-start.4 = ((f32[16,1,8192]{2,1,0:T(1,128)}), f32[16,1,8192]{2,1,0:T(1,128)S(1)}, u32[]{:S(2)}, u32[]{:S(2)}) async-start(f32[16,1,8192]{2,1,0:T(1,128)} %reshape.1447), calls=%async_computation.4 | async-start | bytes 1048576 | tf_op jit(solution)/shard_map/all_to_all | solution.py:203
  202.3 23.6 %all-to-all-start.3 = ((f32[16,1,8192]{2,1,0:T(1,128)}), f32[16,1,8192]{2,1,0:T(1,128)S(1)}, u32[]{:S(2)}, u32[]{:S(2)}) async-start(f32[16,1,8192]{2,1,0:T(1,128)} %reshape.1449), calls=%async_computation.3 | async-start | bytes 1048576 | tf_op jit(solution)/shard_map/all_to_all | solution.py:202
  229.8 0.7 copy-start.21
  229.9 0.7 copy-start.22
  230.0 1.0 copy-start.5
  230.1 1.2 copy-start.6
  234.7 5.4 %copy-start.2 = (f32[1,1,64,16,128]{4,2,3,0,1:T(8,128)S(1)}, f32[1,1,64,16,128]{4,2,3,0,1:T(8,128)}, u32[]{:S(2)}) copy-start(f32[1,1,64,16,128]{4,2,3,0,1:T(8,128)} %get-tuple-element.27) | copy-start | bytes 1572868
  235.5 204.1 %all-to-all-start.11 = ((f32[1,1,512,128]{3,1,0,2:T(1,128)}), f32[1,1,512,128]{3,1,0,2:T(1,128)S(1)}, u32[]{:S(2)}, u32[]{:S(2)}) async-start(f32[1,1,512,128]{3,1,0,2:T(1,128)} %bitcast.164), calls=%async_computation.11 | async-start | bytes 524288 | tf_op jit(solution)/shard_map/all_to_all | solution.py:211
  240.0 1.0 copy-start.1
  438.8 13.2 %copy-start.15 = (bf16[1,1,64,2048]{3,1,2,0:T(2,128)(2,1)S(1)}, bf16[1,1,64,2048]{3,1,2,0:T(2,128)(2,1)}, u32[]{:S(2)}) copy-start(bf16[1,1,64,2048]{3,1,2,0:T(2,128)(2,1)} %get-tuple-element.24) | copy-start | bytes 786436
  439.6 30.0 %all-to-all-start.5 = ((f32[1,1,512,128]{3,1,0,2:T(1,128)}), f32[1,1,512,128]{3,1,0,2:T(1,128)S(1)}, u32[]{:S(2)}, u32[]{:S(2)}) async-start(f32[1,1,512,128]{3,1,0,2:T(1,128)} %bitcast.96), calls=%async_computation.5 | async-start | bytes 524288 | tf_op jit(solution)/shard_map/all_to_all | solution.py:210
  456.3 13.3 %copy-start.10 = (bf16[1,16,32,128]{3,2,1,0:T(8,128)(2,1)S(1)}, bf16[1,16,32,128]{3,2,1,0:T(8,128)(2,1)}, u32[]{:S(2)}) copy-start(bf16[1,16,32,128]{3,2,1,0:T(8,128)(2,1)} %param.9) | copy-start | bytes 393220
  456.3 13.3 %copy-start.12 = (bf16[1,16,32,128]{3,2,1,0:T(8,128)(2,1)S(1)}, bf16[1,16,32,128]{3,2,1,0:T(8,128)(2,1)}, u32[]{:S(2)}) copy-start(bf16[1,16,32,128]{3,2,1,0:T(8,128)(2,1)} %param.8) | copy-start | bytes 393220
  456.3 13.2 %copy-start.14 = (bf16[1,16,32,128]{3,2,1,0:T(8,128)(2,1)S(1)}, bf16[1,16,32,128]{3,2,1,0:T(8,128)(2,1)}, u32[]{:S(2)}) copy-start(bf16[1,16,32,128]{3,2,1,0:T(8,128)(2,1)} %param.7) | copy-start | bytes 393220
  469.6 0.7 copy-start.25
where the time goes:
time: 480 us; the launch traced here: 472 us
  blocking collectives  213 us (44%)
  starting transfers between devices  70.3 us (15%)
  other arithmetic  68.7 us (14%)
  waiting for transfers between devices  60.6 us (13%)
  local copies, waits for them, and re-layouts  39.4 us (8%)
  matrix products  19 us (4%)
    psum x1, blocking collectives, shards(): grad_real, grad_imag = lax.psum((grad_real, grad_imag), 'dp')  196 us
    unnamed x5, other arithmetic  39.3 us
    unnamed x66, local copies, waits for them, and re-layouts  17.3 us
    all_to_all x1, blocking collectives, shards(): lax.all_to_all(gated_im, 'col', split_axis=2, concat_axis=3, tiled=True)  16.2 us
    all_to_all x1, starting transfers between devices, shards(): lax.all_to_all(gated, 'row', split_axis=1, concat_axis=2, tiled=True)  15.3 us
    dot_general x12, matrix products, contract(): jnp.einsum('i' + left_form + ',oi' + table_form + '->o' + out_form, stack...  14.8 us
    all_to_all x1, waiting for transfers between devices, shards(): lax.all_to_all(gated, 'row', split_axis=1, concat_axis=2, tiled=True)  12.6 us
    all_to_all x1, waiting for transfers between devices, shards(): lax.all_to_all(mixed, 'row', split_axis=1, concat_axis=2, tiled=True)  12.3 us
  transfers between devices with their start and end apart: 11, of which 6 were waited for; matrix products, arithmetic and copies ran while one was open for 15% of the time, Pallas kernels for 0%

commit v1 on v0

v1 whole, which is shorter than its diff:
```python
import functools
import math

import jax
import jax.numpy as jnp
import numpy as np
from jax import lax
from jax.experimental import pallas as pl
from jax.experimental.pallas import tpu as pltpu
from jax.sharding import PartitionSpec as P

MESH = pl.DeviceIdType.MESH
BF16 = jnp.bfloat16
F32 = jnp.float32


def split_table(table):
    high = table.astype(np.float32).astype(BF16)
    low = (table - high.astype(np.float64)).astype(np.float32).astype(BF16)
    return high, low


def make_tables(rows_total, cols_total, col_devices):
    half = rows_total // 2
    span = cols_total // col_devices
    keep = rows_total // col_devices
    total = rows_total * cols_total
    freq = np.arange(rows_total).reshape(col_devices, 1, keep, 1)
    angle = 2 * np.pi / rows_total * (freq * np.arange(half) % rows_total)
    row_table = np.concatenate([np.cos(angle), -np.sin(angle)], axis=1)
    row_table = row_table.reshape(col_devices, 2 * keep, half)
    forward_high, forward_low = split_table(row_table)
    inverse_rows = (row_table.reshape(rows_total * 2, half).T / total).astype(np.float32).astype(BF16)
    angle = 2 * np.pi / total * (np.arange(rows_total)[:, None] * np.arange(span) % total)
    twist = np.stack([np.cos(angle), -np.sin(angle)]).astype(np.float32)
    lanes = np.arange(128)
    angle = 2 * np.pi / total * (np.arange(rows_total)[:, None] * lanes * span % total)
    place = np.stack([np.cos(angle), -np.sin(angle)]).astype(np.float32)
    angle = 2 * np.pi / cols_total * (np.arange(col_devices)[:, None] * np.arange(span) % cols_total)
    inner = np.stack([np.cos(angle), -np.sin(angle)]).astype(np.float32)
    angle = 2 * np.pi / span * (np.arange(span)[:, None] * np.arange(span) % span)
    cosine, sine = np.cos(angle), np.sin(angle)
    lane_high, lane_low = split_table(np.block([[cosine, -sine], [sine, cosine]]))
    lane_inverse = np.block([[cosine, sine], [-sine, cosine]]).astype(np.float32).astype(BF16)
    order = np.arange(cols_total).reshape(span, col_devices).T.reshape(-1)
    shuffle = np.zeros((cols_total, cols_total), np.float32)
    shuffle[order, np.arange(cols_total)] = 1
    return dict(
        forward_high=forward_high,
        forward_low=forward_low,
        inverse_rows=inverse_rows,
        twist=twist,
        place=place,
        inner=inner,
        lane_high=lane_high,
        lane_low=lane_low,
        lane_inverse=lane_inverse,
        shuffle=shuffle.astype(BF16),
        unshuffle=shuffle.T.astype(BF16),
    )


def times(a, b, cos_part, sin_part):
    return a * cos_part - b * sin_part, a * sin_part + b * cos_part


def small_fft(values, sign):
    n = len(values)
    if n == 1:
        return values
    if n == 2:
        (a, b), (c, d) = values
        return [(a + c, b + d), (a - c, b - d)]
    if n == 4:
        (a, b), (c, d), (e, f), (g, h) = values
        s0r, s0i, d0r, d0i = a + e, b + f, a - e, b - f
        s1r, s1i, d1r, d1i = c + g, d + h, c - g, d - h
        tr, ti = (-d1i, d1r) if sign > 0 else (d1i, -d1r)
        return [
            (s0r + s1r, s0i + s1i),
            (d0r + tr, d0i + ti),
            (s0r - s1r, s0i - s1i),
            (d0r - tr, d0i - ti),
        ]
    radix = 4 if n % 4 == 0 else 2
    other = n // radix
    out = [None] * n
    parts = []
    for b in range(radix):
        part = small_fft(values[b::radix], sign)
        turned = []
        for k, (re, im) in enumerate(part):
            turn = (b * k) % n
            if turn == 0:
                turned.append((re, im))
            elif 4 * turn == n:
                turned.append((-im, re) if sign > 0 else (im, -re))
            elif 8 * turn == n or 8 * turn == 3 * n:
                w = math.sqrt(0.5)
                c = w if 8 * turn == n else -w
                s = sign * w
                turned.append(times(re, im, c, s))
            else:
                angle = sign * 2 * math.pi * turn / n
                turned.append(times(re, im, math.cos(angle), math.sin(angle)))
        parts.append(turned)
    for k in range(other):
        column = small_fft([parts[b][k] for b in range(radix)], sign)
        for m in range(radix):
            out[k + other * m] = column[m]
    return out


def ring_order(size):
    return sorted(range(1, size), key=lambda s: -min(s, size - s))


def kernel(
    dims,
    gq, gk, vi, go, spec, gain,
    fwd_high_hbm, fwd_low_hbm, inv_hbm, twist_hbm, place_hbm, inner, lane_high, lane_low, lane_inv,
    shuffle_hbm, unshuffle_hbm,
    grad_query, grad_key, grad_value, filter_grad,
    fwd_high, fwd_low, inv_rows, twist, place, shuffle, unshuffle,
    prod, recv1, send2, recv2, send3, recv3, send4, recv4,
    stage, wide, spectra, sint, turned, fsend, frecv,
    load_sem, own_sem, s1, r1, s2, r2, s3, r3, s4, r4, sf, rf,
):
    row_devices, col_devices, keep, span, rows_here = dims
    me_row = lax.axis_index("row")
    me_col = lax.axis_index("col")
    me_dp = lax.axis_index("dp")
    other_dp = 1 - me_dp
    block = 2 * keep
    rows_total = col_devices * keep
    half = rows_total // 2

    barrier = pltpu.get_barrier_semaphore()
    for s in range(1, row_devices):
        pl.semaphore_signal(
            barrier, inc=1, device_id={"row": lax.rem(me_row + s, row_devices)}, device_id_type=MESH
        )
    for s in range(1, col_devices):
        pl.semaphore_signal(
            barrier, inc=1, device_id={"col": lax.rem(me_col + s, col_devices)}, device_id_type=MESH
        )
    pl.semaphore_signal(barrier, inc=1, device_id={"dp": other_dp}, device_id_type=MESH)

    loads = [
        (shuffle_hbm, shuffle),
        (fwd_high_hbm, fwd_high),
        (fwd_low_hbm, fwd_low),
        (twist_hbm, twist),
        (place_hbm, place),
        (inv_hbm, inv_rows),
        (unshuffle_hbm, unshuffle),
    ]
    loads = [
        pltpu.make_async_copy(src, dst, load_sem.at[i]) for i, (src, dst) in enumerate(loads)
    ]
    for copy in loads:
        copy.start()

    prod[0] = (gk[...].astype(F32) * vi[...].astype(F32)).astype(BF16)
    prod[1] = (go[...].astype(F32) * gq[...].astype(F32)).astype(BF16)
    pl.semaphore_wait(barrier, row_devices + col_devices - 1)

    def exchange(axis, me, size, a, send, recv, send_sem, recv_sem, index):
        return pltpu.make_async_remote_copy(
            src_ref=send.at[a, index],
            dst_ref=recv.at[a, me],
            send_sem=send_sem.at[a, index],
            recv_sem=recv_sem.at[a, me],
            device_id={axis: index},
            device_id_type=MESH,
        )

    def own(me, a, send, recv, step):
        return pltpu.make_async_copy(send.at[a, me], recv.at[a, me], own_sem.at[step, a])

    def wait_recv(axis, me, size, a, send, recv, send_sem, recv_sem, step):
        def body(s, carry):
            source = lax.rem(me + s, size)
            pltpu.make_async_remote_copy(
                src_ref=send.at[a, source],
                dst_ref=recv.at[a, source],
                send_sem=send_sem.at[a, source],
                recv_sem=recv_sem.at[a, source],
                device_id={axis: source},
                device_id_type=MESH,
            ).wait_recv()
            return carry

        lax.fori_loop(1, size, body, 0)
        own(me, a, send, recv, step).wait()

    def wait_send(axis, me, size, a, send, recv, send_sem, recv_sem):
        def body(s, carry):
            exchange(axis, me, size, a, send, recv, send_sem, recv_sem, lax.rem(me + s, size)).wait_send()
            return carry

        lax.fori_loop(1, size, body, 0)

    row = ("row", me_row, row_devices)
    col = ("col", me_col, col_devices)

    for a in range(2):
        for s in ring_order(row_devices):
            exchange(*row, a, prod, recv1, s1, r1, lax.rem(me_row + s, row_devices)).start()
        own(me_row, a, prod, recv1, 0).start()

    loads[0].wait()
    planes = spec.shape[0] * spec.shape[1]
    internal = jnp.dot(
        spec[...].reshape(planes, spec.shape[2]), shuffle[...], preferred_element_type=F32
    )
    for k in range(col_devices):
        sint[0, k] = internal[:keep, k * span : (k + 1) * span]
        sint[1, k] = internal[keep:, k * span : (k + 1) * span]

    for i in range(1, 6):
        loads[i].wait()
    for c in range(col_devices):
        rows = pl.ds(c * keep, keep)
        lane = lax.broadcasted_iota(jnp.int32, (keep, 128), 1) == me_col
        pr = jnp.sum(jnp.where(lane, place[0, rows], 0.0), axis=1, keepdims=True)
        pi = jnp.sum(jnp.where(lane, place[1, rows], 0.0), axis=1, keepdims=True)
        tr, ti = times(twist[0, rows], twist[1, rows], pr, pi)
        turned[0, c] = tr
        turned[1, c] = ti

    def row_stage(a):
        wait_recv(*row, a, prod, recv1, s1, r1, 0)
        tokens = recv1[a].reshape(half, span)

        def body(s, carry):
            d = lax.rem(me_col + 1 + s, col_devices)
            z = jnp.dot(fwd_high[d], tokens, preferred_element_type=F32)
            z = z + jnp.dot(fwd_low[d], tokens, preferred_element_type=F32)
            re, im = times(z[:keep], z[keep:], turned[0, d], turned[1, d])
            send2[a, d] = jnp.concatenate([re, im], axis=0).astype(BF16)

            @pl.when(s < col_devices - 1)
            def _():
                exchange(*col, a, send2, recv2, s2, r2, d).start()

            return carry

        lax.fori_loop(0, col_devices, body, 0)
        own(me_col, a, send2, recv2, 1).start()

    def col_stage(a):
        wait_recv(*col, a, send2, recv2, s2, r2, 1)

        def widen(c, carry):
            stage[c] = recv2[a, c].astype(F32)
            return carry

        lax.fori_loop(0, col_devices, widen, 0)

        def forward(t, carry):
            re_rows = pl.ds(pl.multiple_of(t * 8, 8), 8)
            im_rows = pl.ds(pl.multiple_of(keep + t * 8, 8), 8)
            values = [(stage[c, re_rows], stage[c, im_rows]) for c in range(col_devices)]
            values = small_fft(values, -1)
            for k, (re, im) in enumerate(values):
                if k:
                    re, im = times(re, im, inner[0, k : k + 1], inner[1, k : k + 1])
                wide[k, re_rows, :span] = re
                wide[k, re_rows, span:] = im
            return carry

        lax.fori_loop(0, keep // 8, forward, 0)

        def middle(k, carry):
            y = wide[k].astype(BF16)
            x = jnp.dot(y, lane_high[...], preferred_element_type=F32)
            x = x + jnp.dot(y, lane_low[...], preferred_element_type=F32)
            spectra[a, k] = x
            sr, si = sint[0, k], sint[1, k]
            if a == 1:
                si = -si
            re, im = times(x[:, :span], x[:, span:], sr, si)
            v = jnp.concatenate([re, im], axis=1).astype(BF16)
            w = jnp.dot(v, lane_inv[...], preferred_element_type=F32)
            re, im = times(w[:, :span], w[:, span:], inner[0, pl.ds(k, 1)], -inner[1, pl.ds(k, 1)])
            wide[k, :, :span] = re
            wide[k, :, span:] = im
            return carry

        lax.fori_loop(0, col_devices, middle, 0)

        def backward(t, carry):
            re_rows = pl.ds(pl.multiple_of(t * 8, 8), 8)
            im_rows = pl.ds(pl.multiple_of(keep + t * 8, 8), 8)
            values = [(wide[k, re_rows, :span], wide[k, re_rows, span:]) for k in range(col_devices)]
            values = small_fft(values, 1)
            for c, (re, im) in enumerate(values):
                stage[c, re_rows] = re
                stage[c, im_rows] = im
            return carry

        lax.fori_loop(0, keep // 8, backward, 0)

        def narrow(s, carry):
            d = lax.rem(me_col + 1 + s, col_devices)
            send3[a, d] = stage[d].astype(BF16)

            @pl.when(s < col_devices - 1)
            def _():
                exchange(*col, a, send3, recv3, s3, r3, d).start()

            return carry

        lax.fori_loop(0, col_devices, narrow, 0)
        own(me_col, a, send3, recv3, 2).start()

    def back_stage(a):
        wait_recv(*col, a, send3, recv3, s3, r3, 2)
        total = None
        group = max(1, col_devices // 4)
        for g in range(0, col_devices, group):
            parts = []
            for c in range(g, g + group):
                got = recv3[a, c].astype(F32)
                re, im = times(got[:keep], got[keep:], turned[0, c], -turned[1, c])
                parts += [re, im]
            w = jnp.concatenate(parts, axis=0).astype(BF16)
            term = jnp.dot(
                inv_rows[:, g * block : (g + group) * block], w, preferred_element_type=F32
            )
            total = term if total is None else total + term
        send4[a] = total.astype(BF16).reshape(row_devices, rows_here, span)
        for s in ring_order(row_devices):
            exchange(*row, a, send4, recv4, s4, r4, lax.rem(me_row + s, row_devices)).start()
        own(me_row, a, send4, recv4, 3).start()

    row_stage(0)
    row_stage(1)
    col_stage(0)
    col_stage(1)

    scale = 1.0 / (rows_total * col_devices * span)
    for k in range(col_devices):
        m, g = spectra[0, k], spectra[1, k]
        mr, mi, gr, gi = m[:, :span], m[:, span:], g[:, :span], g[:, span:]
        both = jnp.concatenate([mr * gr + mi * gi, mr * gi - mi * gr], axis=0) * scale
        fsend[:, k * span : (k + 1) * span] = both.astype(BF16)
    fcopy = pltpu.make_async_remote_copy(
        src_ref=fsend,
        dst_ref=frecv,
        send_sem=sf,
        recv_sem=rf,
        device_id={"dp": other_dp},
        device_id_type=MESH,
    )
    fcopy.start()

    back_stage(0)
    back_stage(1)

    fcopy.wait_recv()
    loads[6].wait()
    fsum = (fsend[...].astype(F32) + frecv[...].astype(F32)).astype(BF16)
    natural = jnp.dot(fsum, unshuffle[...], preferred_element_type=F32).astype(BF16)
    filter_grad[...] = natural.reshape(filter_grad.shape)

    wait_recv(*row, 0, send4, recv4, s4, r4, 3)
    for c in range(row_devices):
        wide_gain = gain[c]
        conv = recv4[0, c].astype(F32) + wide_gain * prod[0, c].astype(F32)
        grad_query[c] = (go[c].astype(F32) * conv).astype(BF16)
    wait_recv(*row, 1, send4, recv4, s4, r4, 3)
    for c in range(row_devices):
        wide_gain = gain[c]
        mixed_grad = recv4[1, c].astype(F32) + wide_gain * prod[1, c].astype(F32)
        grad_key[c] = (mixed_grad * vi[c].astype(F32)).astype(BF16)
        grad_value[c] = (mixed_grad * gk[c].astype(F32)).astype(BF16)

    for a in range(2):
        wait_send(*row, a, prod, recv1, s1, r1)
        wait_send(*col, a, send2, recv2, s2, r2)
        wait_send(*col, a, send3, recv3, s3, r3)
        wait_send(*row, a, send4, recv4, s4, r4)
    fcopy.wait_send()


def shards(tables, row_devices, col_devices, gate_query, gate_key, value_input, grad_output, filter_spec, skip_gain):
    _, channels, rows_here, span = gate_query.shape
    keep = filter_spec.shape[2]
    cols_total = filter_spec.shape[3]
    rows_total = keep * col_devices
    half = rows_total // 2
    block = 2 * keep
    dims = (row_devices, col_devices, keep, span, rows_here)
    vmem = pl.BlockSpec(memory_space=pltpu.VMEM)
    anywhere = pl.BlockSpec(memory_space=pl.ANY)
    token = jax.ShapeDtypeStruct((channels, rows_here, span), BF16)
    names = [
        "forward_high", "forward_low", "inverse_rows", "twist", "place",
        "inner", "lane_high", "lane_low", "lane_inverse", "shuffle", "unshuffle",
    ]
    small = {"inner", "lane_high", "lane_low", "lane_inverse"}
    dma = pltpu.SemaphoreType.DMA
    tok = (2, row_devices, rows_here, span)
    mid = (2, col_devices, block, span)
    outs = pl.pallas_call(
        functools.partial(kernel, dims),
        out_shape=[token, token, token, jax.ShapeDtypeStruct((2, keep, cols_total), BF16)],
        in_specs=[vmem] * 5
        + [pl.BlockSpec(memory_space=pltpu.SMEM)]
        + [vmem if name in small else anywhere for name in names],
        out_specs=[vmem] * 4,
        scratch_shapes=[
            pltpu.VMEM((col_devices, block, half), BF16),
            pltpu.VMEM((col_devices, block, half), BF16),
            pltpu.VMEM((half, col_devices * block), BF16),
            pltpu.VMEM((2, rows_total, span), F32),
            pltpu.VMEM((2, rows_total, 128), F32),
            pltpu.VMEM((cols_total, cols_total), BF16),
            pltpu.VMEM((cols_total, cols_total), BF16),
            pltpu.VMEM(tok, BF16),
            pltpu.VMEM(tok, BF16),
            pltpu.VMEM(mid, BF16),
            pltpu.VMEM(mid, BF16),
            pltpu.VMEM(mid, BF16),
            pltpu.VMEM(mid, BF16),
            pltpu.VMEM(tok, BF16),
            pltpu.VMEM(tok, BF16),
            pltpu.VMEM((col_devices, block, span), F32),
            pltpu.VMEM((col_devices, keep, 2 * span), F32),
            pltpu.VMEM((2, col_devices, keep, 2 * span), F32),
            pltpu.VMEM((2, col_devices, keep, span), F32),
            pltpu.VMEM((2, col_devices, keep, span), F32),
            pltpu.VMEM((block, cols_total), BF16),
            pltpu.VMEM((block, cols_total), BF16),
            dma((7,)),
            dma((4, 2)),
            dma((2, row_devices)), dma((2, row_devices)),
            dma((2, col_devices)), dma((2, col_devices)),
            dma((2, col_devices)), dma((2, col_devices)),
            dma((2, row_devices)), dma((2, row_devices)),
            dma, dma,
        ],
        compiler_params=pltpu.CompilerParams(
            collective_id=0, has_side_effects=True, vmem_limit_bytes=56 * 1024 * 1024
        ),
        name="hyena_backward",
    )(
        gate_query[0], gate_key[0], value_input[0], grad_output[0], filter_spec[:, 0], skip_gain,
        *[jnp.asarray(tables[name]) for name in names],
    )
    return (outs[0][None], outs[1][None], outs[2][None], outs[3][:, None])


def solution(mesh):
    row_devices, col_devices = mesh.shape["row"], mesh.shape["col"]
    tokens = P("dp", None, "row", "col")
    freq = P(None, "row", "col", None)

    def run(gate_query, gate_key, value_input, grad_output, filter_spec, skip_gain):
        tables = make_tables(filter_spec.shape[2], filter_spec.shape[3], col_devices)
        return jax.shard_map(
            functools.partial(shards, tables, row_devices, col_devices),
            mesh=mesh,
            in_specs=(tokens, tokens, tokens, tokens, freq, P()),
            out_specs=(tokens, tokens, tokens, freq),
            check_vma=False,
        )(gate_query, gate_key, value_input, grad_output, filter_spec, skip_gain)

    return run
```

time: 480 us -> 84.2 us (0.18)
  the two profiles are of different devices: /device:TPU:32 before, /device:TPU:1 now
where the time goes in v1:
time: 84.2 us; the launch traced here: 83.9 us
  Pallas kernels  76.7 us (91%)
  local copies, waits for them, and re-layouts  6.58 us (8%)
    pallas_call x1, Pallas kernels, shards(): pl.pallas_call(functools.partial(kernel, dims), out_shape=[token, token,...  76.7 us
    unnamed x4, local copies, waits for them, and re-layouts  6.58 us

profile of v1, /device:TPU:1, one launch (start us, length us, event | category | flops | bytes accessed | tf_op | source)
XLA Modules:
  0.0 83.9 jit_solution(7525907377162884417)
XLA Ops:
  0.6 76.7 %hyena_backward.1 = (bf16[16,32,128]{2,1,0:T(8,128)(2,1)}, bf16[16,32,128]{2,1,0:T(8,128)(2,1)}, bf16[16,32,128]{2,1,0:T(8,128)(2,1)}, bf16[2,64,2048]{2,1,0:T(8,128)(2,1)}) custom-call(bf16[16,32,128]{2,1,0:T(8,128)(2,1)} %bitcast.13, bf16[16,32,128]{2,1,0:T(8,128)(2,1)} %bitcast.14, bf16[16,32,128]{2,1,0:T(8,128)(2,1)} %bitcast.15, ...), custom_call_target="tpu_custom_call" | custom-call | tf_op jit(solution)/shard_map/hyena_backward/pallas_call | solution.py:407
  77.4 1.6 %copy.26 = bf16[1,16,32,128]{3,2,1,0:T(8,128)(2,1)} copy(bf16[1,16,32,128]{3,2,1,0:T(8,128)(2,1)} %bitcast.19) | data formatting | bytes 262144
  78.9 1.6 %copy.27 = bf16[1,16,32,128]{3,2,1,0:T(8,128)(2,1)} copy(bf16[1,16,32,128]{3,2,1,0:T(8,128)(2,1)} %bitcast.18) | data formatting | bytes 262144
  80.5 1.6 %copy.28 = bf16[1,16,32,128]{3,2,1,0:T(8,128)(2,1)} copy(bf16[1,16,32,128]{3,2,1,0:T(8,128)(2,1)} %bitcast.17) | data formatting | bytes 262144
  82.1 1.9 %copy.29 = bf16[2,1,64,2048]{3,2,1,0:T(8,128)(2,1)} copy(bf16[2,1,64,2048]{3,2,1,0:T(8,128)(2,1)} %bitcast.12) | data formatting | bytes 1048576

commit v2 on v1

v2 whole, which is shorter than its diff:
```python
import functools
import math

import jax
import jax.numpy as jnp
import numpy as np
from jax import lax
from jax.experimental import pallas as pl
from jax.experimental.pallas import tpu as pltpu
from jax.sharding import PartitionSpec as P

MESH = pl.DeviceIdType.MESH
BF16 = jnp.bfloat16
F32 = jnp.float32


def split_table(table):
    high = table.astype(np.float32).astype(BF16)
    low = (table - high.astype(np.float64)).astype(np.float32).astype(BF16)
    return high, low


def make_tables(rows_total, cols_total, col_devices):
    half = rows_total // 2
    span = cols_total // col_devices
    keep = rows_total // col_devices
    total = rows_total * cols_total
    act = keep // 2 + 8
    freq = keep * np.arange(col_devices)[:, None] + np.arange(act)
    angle = 2 * np.pi / rows_total * (freq[:, None, :, None] * np.arange(half) % rows_total)
    row_table = np.concatenate([np.cos(angle), -np.sin(angle)], axis=1)
    row_table[:, :, keep // 2 + 1 :] = 0
    row_table = row_table.reshape(col_devices * 2 * act, half)
    group = math.gcd(col_devices, 4)
    forward_high, forward_low = split_table(row_table.reshape(-1, group * 2 * act, half))
    inverse_rows = (row_table.T / total).astype(np.float32).astype(BF16)
    freq = freq.reshape(-1, 1)
    flip_lanes = np.eye(span)[::-1].astype(np.float32).astype(BF16)
    flip_rows = np.zeros((2, act, 2, keep // 2), np.float32)
    for r in range(1, keep // 2):
        flip_rows[0, r, 0, keep // 2 - r] = 1
        flip_rows[1, r, 1, keep // 2 - r] = -1
    flip_rows = flip_rows.reshape(2 * act, keep).astype(BF16)
    angle = 2 * np.pi / total * (freq * np.arange(span) % total)
    twist = np.stack([np.cos(angle), -np.sin(angle)]).astype(np.float32)
    lanes = np.arange(128)
    angle = 2 * np.pi / total * (freq * lanes * span % total)
    place = np.stack([np.cos(angle), -np.sin(angle)]).astype(np.float32)
    angle = 2 * np.pi / cols_total * (np.arange(col_devices)[:, None] * np.arange(span) % cols_total)
    inner = np.stack([np.cos(angle), -np.sin(angle)]).astype(np.float32)
    angle = 2 * np.pi / span * (np.arange(span)[:, None] * np.arange(span) % span)
    cosine, sine = np.cos(angle), np.sin(angle)
    lane_high, lane_low = split_table(np.block([[cosine, -sine], [sine, cosine]]))
    lane_inverse = np.block([[cosine, sine], [-sine, cosine]]).astype(np.float32).astype(BF16)
    return dict(
        forward_high=forward_high,
        forward_low=forward_low,
        inverse_rows=inverse_rows,
        twist=twist,
        place=place,
        inner=inner,
        lane_high=lane_high,
        lane_low=lane_low,
        lane_inverse=lane_inverse,
        flip_lanes=flip_lanes,
        flip_rows=flip_rows,
        unflip_rows=flip_rows.T,
    )


def times(a, b, cos_part, sin_part):
    return a * cos_part - b * sin_part, a * sin_part + b * cos_part


def small_fft(values, sign):
    n = len(values)
    if n == 1:
        return values
    if n == 2:
        (a, b), (c, d) = values
        return [(a + c, b + d), (a - c, b - d)]
    if n == 4:
        (a, b), (c, d), (e, f), (g, h) = values
        s0r, s0i, d0r, d0i = a + e, b + f, a - e, b - f
        s1r, s1i, d1r, d1i = c + g, d + h, c - g, d - h
        tr, ti = (-d1i, d1r) if sign > 0 else (d1i, -d1r)
        return [
            (s0r + s1r, s0i + s1i),
            (d0r + tr, d0i + ti),
            (s0r - s1r, s0i - s1i),
            (d0r - tr, d0i - ti),
        ]
    radix = 4 if n % 4 == 0 else 2
    other = n // radix
    out = [None] * n
    parts = []
    for b in range(radix):
        part = small_fft(values[b::radix], sign)
        turned = []
        for k, (re, im) in enumerate(part):
            turn = (b * k) % n
            if turn == 0:
                turned.append((re, im))
            elif 4 * turn == n:
                turned.append((-im, re) if sign > 0 else (im, -re))
            elif 8 * turn == n or 8 * turn == 3 * n:
                w = math.sqrt(0.5)
                c = w if 8 * turn == n else -w
                s = sign * w
                turned.append(times(re, im, c, s))
            else:
                angle = sign * 2 * math.pi * turn / n
                turned.append(times(re, im, math.cos(angle), math.sin(angle)))
        parts.append(turned)
    for k in range(other):
        column = small_fft([parts[b][k] for b in range(radix)], sign)
        for m in range(radix):
            out[k + other * m] = column[m]
    return out


def ring_order(size):
    return sorted(range(1, size), key=lambda s: -min(s, size - s))


def kernel(
    dims,
    gq_hbm, gk_hbm, vi_hbm, go_hbm, spec_hbm, gain,
    fwd_high_hbm, fwd_low_hbm, inv_hbm, twist_hbm, place_hbm, inner_hbm, lane_high_hbm, lane_low_hbm,
    lane_inv_hbm, flip_lanes_hbm, flip_rows_hbm, unflip_rows_hbm,
    grad_query_hbm, grad_key_hbm, grad_value_hbm, filter_grad_hbm,
    gq, gk, vi, go, spec,
    fwd_high, fwd_low, inv_rows, twist, place, inner, lane_high, lane_low,
    lane_inv, flip_lanes, flip_rows, unflip_rows,
    grad_query, grad_key, grad_value, filter_grad, flip,
    prod, recv1, send2, recv2, send3, recv3, send4, recv4,
    stage, wide, spectra, smir, sint, turned, fsend, frecv, fown, fmsend, fmrecv,
    load_sem, out_sem, own_sem, s1, r1, s2, r2, s3, r3, s4, r4, sf, rf, sfm, rfm, sm, rm,
):
    row_devices, col_devices, keep, span, rows_here = dims
    me_row = lax.axis_index("row")
    me_col = lax.axis_index("col")
    me_dp = lax.axis_index("dp")
    other_dp = 1 - me_dp
    act = keep // 2 + 8
    block = 2 * act
    rows_total = col_devices * keep
    half = rows_total // 2

    barrier = pltpu.get_barrier_semaphore()
    for s in range(1, row_devices):
        pl.semaphore_signal(
            barrier, inc=1, device_id={"row": lax.rem(me_row + s, row_devices)}, device_id_type=MESH
        )
    for s in range(1, col_devices):
        pl.semaphore_signal(
            barrier, inc=1, device_id={"col": lax.rem(me_col + s, col_devices)}, device_id_type=MESH
        )
    pl.semaphore_signal(barrier, inc=1, device_id={"dp": other_dp}, device_id_type=MESH)

    loads = [
        (gk_hbm, gk), (vi_hbm, vi), (go_hbm, go), (gq_hbm, gq), (spec_hbm, spec),
        (twist_hbm, twist), (place_hbm, place),
        (fwd_high_hbm, fwd_high), (fwd_low_hbm, fwd_low),
        (flip_lanes_hbm, flip_lanes), (flip_rows_hbm, flip_rows), (unflip_rows_hbm, unflip_rows),
        (inner_hbm, inner), (lane_high_hbm, lane_high), (lane_low_hbm, lane_low), (lane_inv_hbm, lane_inv),
        (inv_hbm, inv_rows),
    ]
    loads = [
        pltpu.make_async_copy(src, dst, load_sem.at[i]) for i, (src, dst) in enumerate(loads)
    ]
    for copy in loads:
        copy.start()

    def exchange(axis, me, size, a, send, recv, send_sem, recv_sem, index):
        return pltpu.make_async_remote_copy(
            src_ref=send.at[a, index],
            dst_ref=recv.at[a, me],
            send_sem=send_sem.at[a, index],
            recv_sem=recv_sem.at[a, me],
            device_id={axis: index},
            device_id_type=MESH,
        )

    def own(me, a, send, recv, step):
        return pltpu.make_async_copy(send.at[a, me], recv.at[a, me], own_sem.at[step, a])

    def wait_recv(axis, me, size, a, send, recv, send_sem, recv_sem, step):
        def body(s, carry):
            source = lax.rem(me + s, size)
            pltpu.make_async_remote_copy(
                src_ref=send.at[a, source],
                dst_ref=recv.at[a, source],
                send_sem=send_sem.at[a, source],
                recv_sem=recv_sem.at[a, source],
                device_id={axis: source},
                device_id_type=MESH,
            ).wait_recv()
            return carry

        lax.fori_loop(1, size, body, 0)
        own(me, a, send, recv, step).wait()

    def wait_send(axis, me, size, a, send, recv, send_sem, recv_sem):
        def body(s, carry):
            exchange(axis, me, size, a, send, recv, send_sem, recv_sem, lax.rem(me + s, size)).wait_send()
            return carry

        lax.fori_loop(1, size, body, 0)

    row = ("row", me_row, row_devices)
    col = ("col", me_col, col_devices)

    for a, (left, right) in enumerate([(gk, vi), (go, gq)]):
        loads[2 * a].wait()
        loads[2 * a + 1].wait()
        prod[a] = (left[...].astype(F32) * right[...].astype(F32)).astype(BF16)
        if a == 0:
            pl.semaphore_wait(barrier, row_devices + col_devices - 1)
        for s in ring_order(row_devices):
            exchange(*row, a, prod, recv1, s1, r1, lax.rem(me_row + s, row_devices)).start()
        own(me_row, a, prod, recv1, 0).start()

    loads[4].wait()
    partner = {"col": col_devices - 1 - me_col}
    mirror = pltpu.make_async_remote_copy(
        src_ref=spec.at[:, pl.ds(keep // 2, keep // 2)],
        dst_ref=smir,
        send_sem=sm,
        recv_sem=rm,
        device_id=partner,
        device_id_type=MESH,
    )
    mirror.start()

    loads[5].wait()
    loads[6].wait()
    for c in range(col_devices):
        rows = pl.ds(c * act, act)
        lane = lax.broadcasted_iota(jnp.int32, (act, 128), 1) == me_col
        pr = jnp.sum(jnp.where(lane, place[0, rows], 0.0), axis=1, keepdims=True)
        pi = jnp.sum(jnp.where(lane, place[1, rows], 0.0), axis=1, keepdims=True)
        tr, ti = times(twist[0, rows], twist[1, rows], pr, pi)
        turned[0, c] = tr
        turned[1, c] = ti

    def spectrum_stage():
        mirror.wait_recv()
        loads[9].wait()
        loads[10].wait()
        for t in range(col_devices):
            lanes = slice(t * span, (t + 1) * span)
            far = slice((col_devices - 1 - t) * span, (col_devices - t) * span)
            got = smir[:, :, far].reshape(keep, span)
            got = jnp.dot(got, flip_lanes[...], preferred_element_type=F32).astype(BF16)
            got = jnp.dot(flip_rows[...], got, preferred_element_type=F32)
            tile = spec[:, :, lanes].astype(F32)[:, :act].reshape(block, span)
            flip[lanes, :block] = (tile + got).T
        for k in range(col_devices):
            tile = flip[pl.ds(k, span, stride=col_devices), :block].T
            sint[0, k] = tile[:act]
            sint[1, k] = tile[act:]

    def row_stage(a):
        wait_recv(*row, a, prod, recv1, s1, r1, 0)
        tokens = recv1[a].reshape(half, span)

        groups = fwd_high.shape[0]
        group = col_devices // groups

        def body(s, carry):
            g = lax.rem(lax.div(me_col, group) + 1 + s, groups)
            z = jnp.dot(fwd_high[g], tokens, preferred_element_type=F32)
            z = z + jnp.dot(fwd_low[g], tokens, preferred_element_type=F32)
            for i in range(group):
                d = g * group + i
                zr = z[i * block : i * block + act]
                zi = z[i * block + act : (i + 1) * block]
                re, im = times(zr, zi, turned[0, d], turned[1, d])
                send2[a, d] = jnp.concatenate([re, im], axis=0).astype(BF16)

                @pl.when(d != me_col)
                def _():
                    exchange(*col, a, send2, recv2, s2, r2, d).start()

            return carry

        lax.fori_loop(0, groups, body, 0)
        own(me_col, a, send2, recv2, 1).start()

    def col_stage(a):
        wait_recv(*col, a, send2, recv2, s2, r2, 1)

        def widen(c, carry):
            stage[c] = recv2[a, c].astype(F32)
            return carry

        lax.fori_loop(0, col_devices, widen, 0)

        def forward(t, carry):
            re_rows = pl.ds(pl.multiple_of(t * 8, 8), 8)
            im_rows = pl.ds(pl.multiple_of(act + t * 8, 8), 8)
            values = [(stage[c, re_rows], stage[c, im_rows]) for c in range(col_devices)]
            values = small_fft(values, -1)
            for k, (re, im) in enumerate(values):
                if k:
                    re, im = times(re, im, inner[0, k : k + 1], inner[1, k : k + 1])
                wide[k, re_rows, :span] = re
                wide[k, re_rows, span:] = im
            return carry

        lax.fori_loop(0, act // 8, forward, 0)

        group = math.gcd(col_devices, 8)

        def middle(g, carry):
            some = pl.ds(g * group, group)
            y = wide[some].reshape(group * act, 2 * span).astype(BF16)
            x = jnp.dot(y, lane_high[...], preferred_element_type=F32)
            x = x + jnp.dot(y, lane_low[...], preferred_element_type=F32)
            spectra[a, some] = x.reshape(group, act, 2 * span)
            sr = sint[0, some].reshape(group * act, span)
            si = sint[1, some].reshape(group * act, span)
            if a == 1:
                si = -si
            re, im = times(x[:, :span], x[:, span:], sr, si)
            v = jnp.concatenate([re, im], axis=1).astype(BF16)
            w = jnp.dot(v, lane_inv[...], preferred_element_type=F32)
            w = w.reshape(group, act, 2 * span)
            ir, ii = inner[0, some], inner[1, some]
            re, im = times(w[:, :, :span], w[:, :, span:], ir[:, None], -ii[:, None])
            wide[some, :, :span] = re
            wide[some, :, span:] = im
            return carry

        lax.fori_loop(0, col_devices // group, middle, 0)

        def backward(t, carry):
            re_rows = pl.ds(pl.multiple_of(t * 8, 8), 8)
            im_rows = pl.ds(pl.multiple_of(act + t * 8, 8), 8)
            values = [(wide[k, re_rows, :span], wide[k, re_rows, span:]) for k in range(col_devices)]
            values = small_fft(values, 1)
            for c, (re, im) in enumerate(values):
                stage[c, re_rows] = re
                stage[c, im_rows] = im
            return carry

        lax.fori_loop(0, act // 8, backward, 0)

        def narrow(s, carry):
            d = lax.rem(me_col + 1 + s, col_devices)
            send3[a, d] = stage[d].astype(BF16)

            @pl.when(s < col_devices - 1)
            def _():
                exchange(*col, a, send3, recv3, s3, r3, d).start()

            return carry

        lax.fori_loop(0, col_devices, narrow, 0)
        own(me_col, a, send3, recv3, 2).start()

    def back_stage(a):
        wait_recv(*col, a, send3, recv3, s3, r3, 2)
        parts = []
        for c in range(col_devices):
            got = recv3[a, c].astype(F32)
            re, im = times(got[:act], got[act:], turned[0, c], -turned[1, c])
            parts += [re, im]
        w = jnp.concatenate(parts, axis=0).astype(BF16)
        total = jnp.dot(inv_rows[...], w, preferred_element_type=F32)
        send4[a] = total.astype(BF16).reshape(row_devices, rows_here, span)
        for s in ring_order(row_devices):
            exchange(*row, a, send4, recv4, s4, r4, lax.rem(me_row + s, row_devices)).start()
        own(me_row, a, send4, recv4, 3).start()

    loads[7].wait()
    loads[8].wait()
    row_stage(0)
    spectrum_stage()
    row_stage(1)
    for i in range(12, 16):
        loads[i].wait()
    col_stage(0)
    col_stage(1)

    scale = 1.0 / (rows_total * col_devices * span)
    chunk = math.gcd(col_devices, 4)
    fcopies = []
    for i in range(0, col_devices, chunk):
        for k in range(i, i + chunk):
            m, g = spectra[0, k], spectra[1, k]
            mr, mi, gr, gi = m[:, :span], m[:, span:], g[:, :span], g[:, span:]
            both = jnp.concatenate([mr * gr + mi * gi, mr * gi - mi * gr], axis=0) * scale
            fsend[k] = both.astype(BF16)
        fcopy = pltpu.make_async_remote_copy(
            src_ref=fsend.at[pl.ds(i, chunk)],
            dst_ref=frecv.at[pl.ds(i, chunk)],
            send_sem=sf.at[i // chunk],
            recv_sem=rf.at[i // chunk],
            device_id={"dp": other_dp},
            device_id_type=MESH,
        )
        fcopy.start()
        fcopies.append(fcopy)

    loads[16].wait()
    back_stage(0)
    back_stage(1)

    loads[11].wait()
    fmcopies = []
    for i in range(0, col_devices, chunk):
        fcopies[i // chunk].wait_recv()
        some = pl.ds(i, chunk)
        both = fsend[some].astype(F32) + frecv[some].astype(F32)
        both = both.reshape(chunk * block, span).astype(BF16)
        fown[some] = both.reshape(chunk, block, span)
        both = jnp.dot(both, flip_lanes[...], preferred_element_type=F32).astype(BF16)
        for k in range(chunk):
            tile = both[k * block : (k + 1) * block]
            tile = jnp.dot(unflip_rows[...], tile, preferred_element_type=F32)
            fmsend[col_devices - 1 - i - k] = tile.astype(BF16)
        some = pl.ds(col_devices - i - chunk, chunk)
        fmcopy = pltpu.make_async_remote_copy(
            src_ref=fmsend.at[some],
            dst_ref=fmrecv.at[some],
            send_sem=sfm.at[i // chunk],
            recv_sem=rfm.at[i // chunk],
            device_id=partner,
            device_id_type=MESH,
        )
        fmcopy.start()
        fmcopies.append(fmcopy)

    def put(index, src, dst):
        copy = pltpu.make_async_copy(src, dst, out_sem.at[index])
        copy.start()
        return copy

    puts = []
    wait_recv(*row, 0, send4, recv4, s4, r4, 3)
    for c in range(row_devices):
        conv = recv4[0, c].astype(F32) + gain[c] * prod[0, c].astype(F32)
        grad_query[c] = (go[c].astype(F32) * conv).astype(BF16)
    puts.append(put(0, grad_query, grad_query_hbm))

    for k in reversed(range(col_devices)):
        if (k + 1) % chunk == 0:
            fmcopies[(col_devices - 1 - k) // chunk].wait_recv()
        mine, far = fown[k].astype(F32), fmrecv[k].astype(F32)
        pieces = []
        for p in range(2):
            near, rest = mine[p * act : (p + 1) * act], far[p * keep // 2 : (p + 1) * keep // 2]
            pieces += [near[: keep // 2], near[keep // 2 :] + rest[:8], rest[8:]]
        flip[pl.ds(k, span, stride=col_devices), : 2 * keep] = jnp.concatenate(pieces, axis=0).T
    for t in range(col_devices):
        lanes = slice(t * span, (t + 1) * span)
        tile = flip[lanes, : 2 * keep].T.astype(BF16)
        filter_grad[:, :, lanes] = tile.reshape(2, keep, span)
    puts.append(put(1, filter_grad, filter_grad_hbm))

    wait_recv(*row, 1, send4, recv4, s4, r4, 3)
    for c in range(row_devices):
        mixed_grad = recv4[1, c].astype(F32) + gain[c] * prod[1, c].astype(F32)
        grad_key[c] = (mixed_grad * vi[c].astype(F32)).astype(BF16)
        grad_value[c] = (mixed_grad * gk[c].astype(F32)).astype(BF16)
    puts.append(put(2, grad_key, grad_key_hbm))
    puts.append(put(3, grad_value, grad_value_hbm))

    for a in range(2):
        wait_send(*row, a, prod, recv1, s1, r1)
        wait_send(*col, a, send2, recv2, s2, r2)
        wait_send(*col, a, send3, recv3, s3, r3)
        wait_send(*row, a, send4, recv4, s4, r4)
    for copy in fcopies + fmcopies + [mirror]:
        copy.wait_send()
    for copy in puts:
        copy.wait()


def hand_over(*refs):
    sources, results, held, sems = refs[:4], refs[4:8], refs[8:12], refs[12]
    gets = [pltpu.make_async_copy(sources[i], held[i], sems.at[0, i]) for i in range(4)]
    puts = [pltpu.make_async_copy(held[i], results[i], sems.at[1, i]) for i in range(4)]
    for copy in gets:
        copy.start()
    for get, put in zip(gets, puts):
        get.wait()
        put.start()
    for copy in puts:
        copy.wait()


def shards(tables, row_devices, col_devices, gate_query, gate_key, value_input, grad_output, filter_spec, skip_gain):
    _, channels, rows_here, span = gate_query.shape
    keep = filter_spec.shape[2]
    cols_total = filter_spec.shape[3]
    rows_total = keep * col_devices
    half = rows_total // 2
    act = keep // 2 + 8
    dims = (row_devices, col_devices, keep, span, rows_here)
    anywhere = pl.BlockSpec(memory_space=pl.ANY)
    token = jax.ShapeDtypeStruct((channels, rows_here, span), BF16)
    names = [
        "forward_high", "forward_low", "inverse_rows", "twist", "place",
        "inner", "lane_high", "lane_low", "lane_inverse", "flip_lanes", "flip_rows",
        "unflip_rows",
    ]
    dma = pltpu.SemaphoreType.DMA
    tok = (2, row_devices, rows_here, span)
    mid = (2, col_devices, 2 * act, span)
    grad = (col_devices, 2 * act, span)
    mirrored = (col_devices, keep, span)
    freq = jax.ShapeDtypeStruct((2, keep, cols_total), BF16)
    chunks = (math.gcd(col_devices, 4),)
    chunks = (col_devices // chunks[0],)
    outs = pl.pallas_call(
        functools.partial(kernel, dims),
        out_shape=[token, token, token, freq],
        in_specs=[anywhere] * 5 + [pl.BlockSpec(memory_space=pltpu.SMEM)] + [anywhere] * len(names),
        out_specs=[anywhere] * 4,
        scratch_shapes=[pltpu.VMEM(token.shape, BF16)] * 4
        + [pltpu.VMEM(freq.shape, BF16)]
        + [pltpu.VMEM(tables[name].shape, tables[name].dtype) for name in names]
        + [pltpu.VMEM(token.shape, BF16)] * 3
        + [pltpu.VMEM(freq.shape, BF16)]
        + [
            pltpu.VMEM((cols_total, 128), F32),
            pltpu.VMEM(tok, BF16),
            pltpu.VMEM(tok, BF16),
            pltpu.VMEM(mid, BF16),
            pltpu.VMEM(mid, BF16),
            pltpu.VMEM(mid, BF16),
            pltpu.VMEM(mid, BF16),
            pltpu.VMEM(tok, BF16),
            pltpu.VMEM(tok, BF16),
            pltpu.VMEM(grad, F32),
            pltpu.VMEM((col_devices, act, 2 * span), F32),
            pltpu.VMEM((2, col_devices, act, 2 * span), F32),
            pltpu.VMEM((2, keep // 2, cols_total), BF16),
            pltpu.VMEM((2, col_devices, act, span), F32),
            pltpu.VMEM((2, col_devices, act, span), F32),
            pltpu.VMEM(grad, BF16),
            pltpu.VMEM(grad, BF16),
            pltpu.VMEM(grad, BF16),
            pltpu.VMEM(mirrored, BF16),
            pltpu.VMEM(mirrored, BF16),
            dma((17,)),
            dma((4,)),
            dma((4, 2)),
            dma((2, row_devices)), dma((2, row_devices)),
            dma((2, col_devices)), dma((2, col_devices)),
            dma((2, col_devices)), dma((2, col_devices)),
            dma((2, row_devices)), dma((2, row_devices)),
            dma(chunks), dma(chunks),
            dma(chunks), dma(chunks),
            dma, dma,
        ],
        compiler_params=pltpu.CompilerParams(
            collective_id=0, has_side_effects=True, vmem_limit_bytes=56 * 1024 * 1024
        ),
        name="hyena_backward",
    )(
        gate_query[0], gate_key[0], value_input[0], grad_output[0], filter_spec[:, 0], skip_gain,
        *[jnp.asarray(tables[name]) for name in names],
    )
    outs = pl.pallas_call(
        hand_over,
        out_shape=[jax.ShapeDtypeStruct(out.shape, out.dtype) for out in outs],
        in_specs=[anywhere] * 4,
        out_specs=[anywhere] * 4,
        scratch_shapes=[pltpu.VMEM(out.shape, out.dtype) for out in outs] + [dma((2, 4))],
        name="hand_over",
    )(*outs)
    return (outs[0][None], outs[1][None], outs[2][None], outs[3][:, None])


def solution(mesh):
    row_devices, col_devices = mesh.shape["row"], mesh.shape["col"]
    tokens = P("dp", None, "row", "col")
    freq = P(None, "row", "col", None)

    def run(gate_query, gate_key, value_input, grad_output, filter_spec, skip_gain):
        tables = make_tables(filter_spec.shape[2], filter_spec.shape[3], col_devices)
        return jax.shard_map(
            functools.partial(shards, tables, row_devices, col_devices),
            mesh=mesh,
            in_specs=(tokens, tokens, tokens, tokens, freq, P()),
            out_specs=(tokens, tokens, tokens, freq),
            check_vma=False,
        )(gate_query, gate_key, value_input, grad_output, filter_spec, skip_gain)

    return run
```

time: 84.2 us -> 65 us (0.77)
  Pallas kernels: 76.7 us -> 64.2 us
  local copies, waits for them, and re-layouts: 6.58 us -> 0 us
    pallas_call x1, Pallas kernels: 76.7 us -> 62.1 us  [shards(): pl.pallas_call(functools.partial(kernel, dims), out_shape=[token, token,...]
    unnamed x4 -> x0, local copies, waits for them, and re-layouts: 6.58 us -> none
    pallas_call x0 -> x1, Pallas kernels: none -> 2.11 us  [shards(): pl.pallas_call(hand_over, out_shape=[jax.ShapeDtypeStruct(out.shape, out....]
where the time goes in v2:
time: 65 us; the launch traced here: 64.8 us
  Pallas kernels  64.2 us (99%)
    pallas_call x1, Pallas kernels, shards(): pl.pallas_call(functools.partial(kernel, dims), out_shape=[token, token,...  62.1 us
    pallas_call x1, Pallas kernels, shards(): pl.pallas_call(hand_over, out_shape=[jax.ShapeDtypeStruct(out.shape, out....  2.11 us

profile of v2, /device:TPU:1, one launch (start us, length us, event | category | flops | bytes accessed | tf_op | source)
XLA Modules:
  0.0 64.8 jit_solution(119440202891567499)
XLA Ops:
  0.6 62.1 %hyena_backward.1 = (bf16[16,32,128]{2,1,0:T(8,128)(2,1)}, bf16[16,32,128]{2,1,0:T(8,128)(2,1)}, bf16[16,32,128]{2,1,0:T(8,128)(2,1)}, bf16[2,64,2048]{2,1,0:T(8,128)(2,1)}) custom-call(bf16[16,32,128]{2,1,0:T(8,128)(2,1)} %bitcast.12, bf16[16,32,128]{2,1,0:T(8,128)(2,1)} %bitcast.13, bf16[16,32,128]{2,1,0:T(8,128)(2,1)} %bitcast.14, ...), custom_call_target="tpu_custom_call" | custom-call | tf_op jit(solution)/shard_map/hyena_backward/pallas_call | solution.py:518
  62.7 2.1 %hand_over.1 = (bf16[16,32,128]{2,1,0:T(8,128)(2,1)}, bf16[16,32,128]{2,1,0:T(8,128)(2,1)}, bf16[16,32,128]{2,1,0:T(8,128)(2,1)}, bf16[2,64,2048]{2,1,0:T(8,128)(2,1)}) custom-call(bf16[16,32,128]{2,1,0:T(8,128)(2,1)} %get-tuple-element.12.refs_0_, bf16[16,32,128]{2,1,0:T(8,128)(2,1)} %get-tuple-element.13.refs_1_, ...), custom_call_target="tpu_custom_call" | custom-call | tf_op jit(solution)/shard_map/hand_over/pallas_call | solution.py:568

commit v3 on v2

--- a/solution.py
+++ b/solution.py
@@ -176,8 +176,8 @@
         return pltpu.make_async_remote_copy(
             src_ref=send.at[a, index],
             dst_ref=recv.at[a, me],
-            send_sem=send_sem.at[a, index],
-            recv_sem=recv_sem.at[a, me],
+            send_sem=send_sem.at[a],
+            recv_sem=recv_sem.at[a],
             device_id={axis: index},
             device_id_type=MESH,
         )
@@ -186,27 +186,13 @@
         return pltpu.make_async_copy(send.at[a, me], recv.at[a, me], own_sem.at[step, a])
 
     def wait_recv(axis, me, size, a, send, recv, send_sem, recv_sem, step):
-        def body(s, carry):
-            source = lax.rem(me + s, size)
-            pltpu.make_async_remote_copy(
-                src_ref=send.at[a, source],
-                dst_ref=recv.at[a, source],
-                send_sem=send_sem.at[a, source],
-                recv_sem=recv_sem.at[a, source],
-                device_id={axis: source},
-                device_id_type=MESH,
-            ).wait_recv()
-            return carry
-
-        lax.fori_loop(1, size, body, 0)
+        every = recv.at[a, pl.ds(0, size - 1)]
+        pltpu.make_async_copy(every, every, recv_sem.at[a]).wait()
         own(me, a, send, recv, step).wait()
 
     def wait_send(axis, me, size, a, send, recv, send_sem, recv_sem):
-        def body(s, carry):
-            exchange(axis, me, size, a, send, recv, send_sem, recv_sem, lax.rem(me + s, size)).wait_send()
-            return carry
-
-        lax.fori_loop(1, size, body, 0)
+        every = send.at[a, pl.ds(0, size - 1)]
+        pltpu.make_async_copy(every, every, send_sem.at[a]).wait()
 
     row = ("row", me_row, row_devices)
     col = ("col", me_col, col_devices)
@@ -460,6 +446,10 @@
         filter_grad[:, :, lanes] = tile.reshape(2, keep, span)
     puts.append(put(1, filter_grad, filter_grad_hbm))
 
+    for a in range(2):
+        wait_send(*row, a, prod, recv1, s1, r1)
+        wait_send(*col, a, send2, recv2, s2, r2)
+        wait_send(*col, a, send3, recv3, s3, r3)
     wait_recv(*row, 1, send4, recv4, s4, r4, 3)
     for c in range(row_devices):
         mixed_grad = recv4[1, c].astype(F32) + gain[c] * prod[1, c].astype(F32)
@@ -469,9 +459,6 @@
     puts.append(put(3, grad_value, grad_value_hbm))
 
     for a in range(2):
-        wait_send(*row, a, prod, recv1, s1, r1)
-        wait_send(*col, a, send2, recv2, s2, r2)
-        wait_send(*col, a, send3, recv3, s3, r3)
         wait_send(*row, a, send4, recv4, s4, r4)
     for copy in fcopies + fmcopies + [mirror]:
         copy.wait_send()
@@ -549,10 +536,7 @@
             dma((17,)),
             dma((4,)),
             dma((4, 2)),
-            dma((2, row_devices)), dma((2, row_devices)),
-            dma((2, col_devices)), dma((2, col_devices)),
-            dma((2, col_devices)), dma((2, col_devices)),
-            dma((2, row_devices)), dma((2, row_devices)),
+            dma((2,)), dma((2,)), dma((2,)), dma((2,)), dma((2,)), dma((2,)), dma((2,)), dma((2,)),
             dma(chunks), dma(chunks),
             dma(chunks), dma(chunks),
             dma, dma,

time: 65 us -> 61.8 us (0.951)
  Pallas kernels: 64.2 us -> 61 us
    pallas_call x1, Pallas kernels: 62.1 us -> 58.9 us  [shards(): pl.pallas_call(functools.partial(kernel, dims), out_shape=[token, token,...]
where the time goes in v3:
time: 61.8 us; the launch traced here: 61.6 us
  Pallas kernels  61 us (99%)
  between operations  0.64 us (1%)
    pallas_call x1, Pallas kernels, shards(): pl.pallas_call(functools.partial(kernel, dims), out_shape=[token, token,...  58.9 us
    pallas_call x1, Pallas kernels, shards(): pl.pallas_call(hand_over, out_shape=[jax.ShapeDtypeStruct(out.shape, out....  2.11 us

profile of v3, /device:TPU:1, one launch (start us, length us, event | category | flops | bytes accessed | tf_op | source)
XLA Modules:
  0.0 61.6 jit_solution(14283129171815963377)
XLA Ops:
  0.6 58.9 %hyena_backward.1 = (bf16[16,32,128]{2,1,0:T(8,128)(2,1)}, bf16[16,32,128]{2,1,0:T(8,128)(2,1)}, bf16[16,32,128]{2,1,0:T(8,128)(2,1)}, bf16[2,64,2048]{2,1,0:T(8,128)(2,1)}) custom-call(bf16[16,32,128]{2,1,0:T(8,128)(2,1)} %bitcast.12, bf16[16,32,128]{2,1,0:T(8,128)(2,1)} %bitcast.13, bf16[16,32,128]{2,1,0:T(8,128)(2,1)} %bitcast.14, ...), custom_call_target="tpu_custom_call" | custom-call | tf_op jit(solution)/shard_map/hyena_backward/pallas_call | solution.py:505
  59.5 2.1 %hand_over.1 = (bf16[16,32,128]{2,1,0:T(8,128)(2,1)}, bf16[16,32,128]{2,1,0:T(8,128)(2,1)}, bf16[16,32,128]{2,1,0:T(8,128)(2,1)}, bf16[2,64,2048]{2,1,0:T(8,128)(2,1)}) custom-call(bf16[16,32,128]{2,1,0:T(8,128)(2,1)} %get-tuple-element.12.refs_0_, bf16[16,32,128]{2,1,0:T(8,128)(2,1)} %get-tuple-element.13.refs_1_, ...), custom_call_target="tpu_custom_call" | custom-call | tf_op jit(solution)/shard_map/hand_over/pallas_call | solution.py:552

commit v4 on v3

--- a/solution.py
+++ b/solution.py
@@ -25,22 +25,39 @@
     span = cols_total // col_devices
     keep = rows_total // col_devices
     total = rows_total * cols_total
-    act = keep // 2 + 8
-    freq = keep * np.arange(col_devices)[:, None] + np.arange(act)
+    act, wire, middle = keep // 2 + 8, keep // 2, col_devices // 2
+    freq = keep * np.arange(col_devices)[:, None] + np.arange(wire)
+    freq[middle:] += 1
     angle = 2 * np.pi / rows_total * (freq[:, None, :, None] * np.arange(half) % rows_total)
     row_table = np.concatenate([np.cos(angle), -np.sin(angle)], axis=1)
-    row_table[:, :, keep // 2 + 1 :] = 0
-    row_table = row_table.reshape(col_devices * 2 * act, half)
+    row_table[0, 1, 0] = 1.0 - 2.0 * (np.arange(half) % 2)
+    row_table = row_table.reshape(col_devices * keep, half)
     group = math.gcd(col_devices, 4)
-    forward_high, forward_low = split_table(row_table.reshape(-1, group * 2 * act, half))
+    forward_high, forward_low = split_table(row_table.reshape(-1, group * keep, half))
     inverse_rows = (row_table.T / total).astype(np.float32).astype(BF16)
     freq = freq.reshape(-1, 1)
+    angle = np.pi / cols_total * np.arange(cols_total).reshape(col_devices, span)
+    half_twist = np.stack([np.cos(angle), -np.sin(angle)]).astype(np.float32)
     flip_lanes = np.eye(span)[::-1].astype(np.float32).astype(BF16)
-    flip_rows = np.zeros((2, act, 2, keep // 2), np.float32)
-    for r in range(1, keep // 2):
-        flip_rows[0, r, 0, keep // 2 - r] = 1
-        flip_rows[1, r, 1, keep // 2 - r] = -1
-    flip_rows = flip_rows.reshape(2 * act, keep).astype(BF16)
+    own, mir = 0, 2 * keep
+    pick = np.zeros((2, 2 * act, 2 * keep + 2 * wire), np.float32)
+    unpick = np.zeros((2, 2 * wire + 16, 2 * wire), np.float32)
+    merge = np.zeros((2, 2 * keep, 4 * wire), np.float32)
+    for p, sign in enumerate((1, -1)):
+        for i in range(wire):
+            pick[0, p * act + i, own + p * keep + i] = 1
+            pick[1, p * act + i, own + p * keep + i + 1] = 1
+            pick[1, p * act + i, mir + p * wire + wire - 1 - i] = sign
+            unpick[1, p * wire + wire - 1 - i, p * wire + i] = sign
+            merge[0, p * keep + i, p * wire + i] = 1
+            merge[0, p * keep + wire + i, 2 * wire + p * wire + i] = 1
+            merge[1, p * keep + i + 1, p * wire + i] = 1
+            if i:
+                pick[0, p * act + i, mir + p * wire + wire - i] = sign
+                unpick[0, p * wire + wire - i, p * wire + i] = sign
+                merge[1, p * keep + wire + i, 2 * wire + p * wire + i] = 1
+        unpick[0, 2 * wire + p, p * wire] = sign
+    pick, unpick, merge = pick.astype(BF16), unpick.astype(BF16), merge.astype(BF16)
     angle = 2 * np.pi / total * (freq * np.arange(span) % total)
     twist = np.stack([np.cos(angle), -np.sin(angle)]).astype(np.float32)
     lanes = np.arange(128)
@@ -63,8 +80,10 @@
         lane_low=lane_low,
         lane_inverse=lane_inverse,
         flip_lanes=flip_lanes,
-        flip_rows=flip_rows,
-        unflip_rows=flip_rows.T,
+        pick=pick,
+        unpick=unpick,
+        merge=merge,
+        half_twist=half_twist,
     )
 
 
@@ -127,22 +146,23 @@
     dims,
     gq_hbm, gk_hbm, vi_hbm, go_hbm, spec_hbm, gain,
     fwd_high_hbm, fwd_low_hbm, inv_hbm, twist_hbm, place_hbm, inner_hbm, lane_high_hbm, lane_low_hbm,
-    lane_inv_hbm, flip_lanes_hbm, flip_rows_hbm, unflip_rows_hbm,
+    lane_inv_hbm, flip_lanes_hbm, pick_hbm, unpick_hbm, merge_hbm, half_twist_hbm,
     grad_query_hbm, grad_key_hbm, grad_value_hbm, filter_grad_hbm,
     gq, gk, vi, go, spec,
     fwd_high, fwd_low, inv_rows, twist, place, inner, lane_high, lane_low,
-    lane_inv, flip_lanes, flip_rows, unflip_rows,
+    lane_inv, flip_lanes, pick, unpick, merge, half_twist,
     grad_query, grad_key, grad_value, filter_grad, flip,
     prod, recv1, send2, recv2, send3, recv3, send4, recv4,
-    stage, wide, spectra, smir, sint, turned, fsend, frecv, fown, fmsend, fmrecv,
-    load_sem, out_sem, own_sem, s1, r1, s2, r2, s3, r3, s4, r4, sf, rf, sfm, rfm, sm, rm,
+    stage, wide, spectra, smir, sfar, head, sint, turned, fsend, frecv, fown, fmsend, fmrecv, extra, fx,
+    load_sem, out_sem, own_sem, s1, r1, s2, r2, s3, r3, s4, r4, sf, rf, sfm, rfm, sx, rx,
 ):
-    row_devices, col_devices, keep, span, rows_here = dims
+    row_devices, col_devices, keep, span = dims
     me_row = lax.axis_index("row")
     me_col = lax.axis_index("col")
     me_dp = lax.axis_index("dp")
     other_dp = 1 - me_dp
     act = keep // 2 + 8
+    wire = keep // 2
     block = 2 * act
     rows_total = col_devices * keep
     half = rows_total // 2
@@ -156,15 +176,18 @@
         pl.semaphore_signal(
             barrier, inc=1, device_id={"col": lax.rem(me_col + s, col_devices)}, device_id_type=MESH
         )
+    partner = col_devices - 1 - me_col
+    across = {"dp": other_dp, "col": partner}
     pl.semaphore_signal(barrier, inc=1, device_id={"dp": other_dp}, device_id_type=MESH)
+    pl.semaphore_signal(barrier, inc=1, device_id=across, device_id_type=MESH)
 
     loads = [
         (gk_hbm, gk), (vi_hbm, vi), (go_hbm, go), (gq_hbm, gq), (spec_hbm, spec),
         (twist_hbm, twist), (place_hbm, place),
         (fwd_high_hbm, fwd_high), (fwd_low_hbm, fwd_low),
-        (flip_lanes_hbm, flip_lanes), (flip_rows_hbm, flip_rows), (unflip_rows_hbm, unflip_rows),
+        (flip_lanes_hbm, flip_lanes), (pick_hbm, pick), (unpick_hbm, unpick),
         (inner_hbm, inner), (lane_high_hbm, lane_high), (lane_low_hbm, lane_low), (lane_inv_hbm, lane_inv),
-        (inv_hbm, inv_rows),
+        (inv_hbm, inv_rows), (merge_hbm, merge), (half_twist_hbm, half_twist),
     ]
     loads = [
         pltpu.make_async_copy(src, dst, load_sem.at[i]) for i, (src, dst) in enumerate(loads)
@@ -202,28 +225,42 @@
         loads[2 * a + 1].wait()
         prod[a] = (left[...].astype(F32) * right[...].astype(F32)).astype(BF16)
         if a == 0:
-            pl.semaphore_wait(barrier, row_devices + col_devices - 1)
+            pl.semaphore_wait(barrier, row_devices + col_devices)
         for s in ring_order(row_devices):
             exchange(*row, a, prod, recv1, s1, r1, lax.rem(me_row + s, row_devices)).start()
         own(me_row, a, prod, recv1, 0).start()
 
     loads[4].wait()
-    partner = {"col": col_devices - 1 - me_col}
-    mirror = pltpu.make_async_remote_copy(
-        src_ref=spec.at[:, pl.ds(keep // 2, keep // 2)],
-        dst_ref=smir,
-        send_sem=sm,
-        recv_sem=rm,
-        device_id=partner,
-        device_id_type=MESH,
-    )
-    mirror.start()
+    middle = col_devices // 2
+    side = lax.div(me_col, middle)
+    other = jnp.where(lax.rem(me_col, middle) == 0, middle, col_devices) - me_col
+    first = (me_col == 0).astype(F32)
+
+    def send_one(src, dst, index, device):
+        copy = pltpu.make_async_remote_copy(
+            src_ref=src,
+            dst_ref=dst,
+            send_sem=sx.at[index],
+            recv_sem=rx.at[index],
+            device_id=device,
+            device_id_type=MESH,
+        )
+        copy.start()
+        return copy
+
+    mirror = send_one(spec.at[:, pl.ds(wire, wire)], smir, 0, {"col": partner})
+    for t in range(col_devices):
+        heads = spec[:, :, t * span : (t + 1) * span].astype(F32)
+        sfar[2 * t : 2 * t + 1] = heads[0, :1]
+        sfar[2 * t + 1 : 2 * t + 2] = heads[1, :1]
+    head[0] = sfar[...].astype(BF16)
+    mirror_far = send_one(head.at[0], head.at[1], 1, {"col": other})
 
     loads[5].wait()
     loads[6].wait()
     for c in range(col_devices):
-        rows = pl.ds(c * act, act)
-        lane = lax.broadcasted_iota(jnp.int32, (act, 128), 1) == me_col
+        rows = pl.ds(c * wire, wire)
+        lane = lax.broadcasted_iota(jnp.int32, (wire, 128), 1) == me_col
         pr = jnp.sum(jnp.where(lane, place[0, rows], 0.0), axis=1, keepdims=True)
         pi = jnp.sum(jnp.where(lane, place[1, rows], 0.0), axis=1, keepdims=True)
         tr, ti = times(twist[0, rows], twist[1, rows], pr, pi)
@@ -232,16 +269,29 @@
 
     def spectrum_stage():
         mirror.wait_recv()
+        mirror_far.wait_recv()
         loads[9].wait()
         loads[10].wait()
+        low = 1.0 - first - side.astype(F32)
+        sfar[...] = jnp.dot(head[1], flip_lanes[...], preferred_element_type=F32) * low
+        heads = head[1].astype(F32) * first
+        top = lax.broadcasted_iota(jnp.int32, (8, span), 0) == 0
         for t in range(col_devices):
             lanes = slice(t * span, (t + 1) * span)
-            far = slice((col_devices - 1 - t) * span, (col_devices - t) * span)
-            got = smir[:, :, far].reshape(keep, span)
+            away = col_devices - 1 - t
+            back = slice(away * span, (away + 1) * span)
+            got = smir[:, :, back].reshape(2 * wire, span)
             got = jnp.dot(got, flip_lanes[...], preferred_element_type=F32).astype(BF16)
-            got = jnp.dot(flip_rows[...], got, preferred_element_type=F32)
-            tile = spec[:, :, lanes].astype(F32)[:, :act].reshape(block, span)
-            flip[lanes, :block] = (tile + got).T
+            tile = jnp.concatenate([spec[:, :, lanes].reshape(2 * keep, span), got], axis=0)
+            tile = jnp.dot(pick[side], tile, preferred_element_type=F32)
+            pieces = []
+            for p, sign in enumerate((1.0, -1.0)):
+                plane = tile[p * act : (p + 1) * act]
+                turned_head = sign * sfar[2 * away + p : 2 * away + p + 1]
+                pieces.append(jnp.where(top, plane[:8] + turned_head, plane[:8]))
+                pieces.append(plane[8:wire])
+                pieces.append(jnp.where(top, plane[wire:] + heads[2 * t + p : 2 * t + p + 1], plane[wire:]))
+            flip[lanes, :block] = jnp.concatenate(pieces, axis=0).T
         for k in range(col_devices):
             tile = flip[pl.ds(k, span, stride=col_devices), :block].T
             sint[0, k] = tile[:act]
@@ -260,8 +310,8 @@
             z = z + jnp.dot(fwd_low[g], tokens, preferred_element_type=F32)
             for i in range(group):
                 d = g * group + i
-                zr = z[i * block : i * block + act]
-                zi = z[i * block + act : (i + 1) * block]
+                zr = z[i * keep : i * keep + wire]
+                zi = z[i * keep + wire : (i + 1) * keep]
                 re, im = times(zr, zi, turned[0, d], turned[1, d])
                 send2[a, d] = jnp.concatenate([re, im], axis=0).astype(BF16)
 
@@ -278,7 +328,15 @@
         wait_recv(*col, a, send2, recv2, s2, r2, 1)
 
         def widen(c, carry):
-            stage[c] = recv2[a, c].astype(F32)
+            got = recv2[a, c].astype(F32)
+            re, im = got[:wire], got[wire:]
+            row_half = first * im[:1]
+            top = lax.broadcasted_iota(jnp.int32, (8, span), 0) == 0
+            stage[c, :wire] = re
+            stage[c, wire:act] = jnp.where(top, row_half * half_twist[0, pl.ds(c, 1)], 0.0)
+            stage[c, act : act + 8] = jnp.where(top, im[:8] - row_half, im[:8])
+            stage[c, act + 8 : act + wire] = im[8:]
+            stage[c, act + wire :] = jnp.where(top, row_half * half_twist[1, pl.ds(c, 1)], 0.0)
             return carry
 
         lax.fori_loop(0, col_devices, widen, 0)
@@ -335,7 +393,15 @@
 
         def narrow(s, carry):
             d = lax.rem(me_col + 1 + s, col_devices)
-            send3[a, d] = stage[d].astype(BF16)
+            got = stage[d]
+            re, im = got[:wire], got[act : act + wire]
+            row_half = (
+                got[wire : wire + 1] * half_twist[0, pl.ds(d, 1)]
+                + got[act + wire : act + wire + 1] * half_twist[1, pl.ds(d, 1)]
+            )
+            top = lax.broadcasted_iota(jnp.int32, (wire, span), 0) == 0
+            im = jnp.where(top, im + first * (row_half - im), im)
+            send3[a, d] = jnp.concatenate([re, im], axis=0).astype(BF16)
 
             @pl.when(s < col_devices - 1)
             def _():
@@ -351,11 +417,11 @@
         parts = []
         for c in range(col_devices):
             got = recv3[a, c].astype(F32)
-            re, im = times(got[:act], got[act:], turned[0, c], -turned[1, c])
+            re, im = times(got[:wire], got[wire:], turned[0, c], -turned[1, c])
             parts += [re, im]
         w = jnp.concatenate(parts, axis=0).astype(BF16)
         total = jnp.dot(inv_rows[...], w, preferred_element_type=F32)
-        send4[a] = total.astype(BF16).reshape(row_devices, rows_here, span)
+        send4[a] = total.astype(BF16).reshape(row_devices, half // row_devices, span)
         for s in ring_order(row_devices):
             exchange(*row, a, send4, recv4, s4, r4, lax.rem(me_row + s, row_devices)).start()
         own(me_row, a, send4, recv4, 3).start()
@@ -365,59 +431,85 @@
     row_stage(0)
     spectrum_stage()
     row_stage(1)
-    for i in range(12, 16):
+    for i in [12, 13, 14, 15, 18]:
         loads[i].wait()
     col_stage(0)
     col_stage(1)
 
     scale = 1.0 / (rows_total * col_devices * span)
-    chunk = math.gcd(col_devices, 4)
-    fcopies = []
-    for i in range(0, col_devices, chunk):
-        for k in range(i, i + chunk):
-            m, g = spectra[0, k], spectra[1, k]
-            mr, mi, gr, gi = m[:, :span], m[:, span:], g[:, :span], g[:, span:]
-            both = jnp.concatenate([mr * gr + mi * gi, mr * gi - mi * gr], axis=0) * scale
-            fsend[k] = both.astype(BF16)
-        fcopy = pltpu.make_async_remote_copy(
-            src_ref=fsend.at[pl.ds(i, chunk)],
-            dst_ref=frecv.at[pl.ds(i, chunk)],
-            send_sem=sf.at[i // chunk],
-            recv_sem=rf.at[i // chunk],
+    chunks = 4 if col_devices % 4 == 0 else 2
+    chunk = col_devices // chunks
+
+    def part(device, j):
+        return lax.rem(device * (chunks // 2) + j, chunks)
+
+    def fcopy(q):
+        some = pl.ds(q * chunk, chunk)
+        return pltpu.make_async_remote_copy(
+            src_ref=fsend.at[some],
+            dst_ref=frecv.at[some],
+            send_sem=sf.at[q],
+            recv_sem=rf.at[q],
             device_id={"dp": other_dp},
             device_id_type=MESH,
         )
-        fcopy.start()
-        fcopies.append(fcopy)
+
+    for j in range(chunks):
+        q = part(other_dp, j)
+        for i in range(chunk):
+            k = q * chunk + i
+            m, g = spectra[0, k], spectra[1, k]
+            mr, mi, gr, gi = m[:, :span], m[:, span:], g[:, :span], g[:, span:]
+            re, im = (mr * gr + mi * gi) * scale, (mr * gi - mi * gr) * scale
+            fsend[k] = jnp.concatenate([re[:wire], im[:wire]], axis=0).astype(BF16)
+            extra[pl.ds(2 * k, 1)] = re[wire : wire + 1]
+            extra[pl.ds(2 * k + 1, 1)] = im[wire : wire + 1]
+        fcopy(q).start()
+    fx[0] = extra[...].astype(BF16)
+    excopy = send_one(fx.at[0], fx.at[1], 3, {"dp": other_dp})
 
     loads[16].wait()
     back_stage(0)
     back_stage(1)
 
     loads[11].wait()
-    fmcopies = []
-    for i in range(0, col_devices, chunk):
-        fcopies[i // chunk].wait_recv()
-        some = pl.ds(i, chunk)
-        both = fsend[some].astype(F32) + frecv[some].astype(F32)
-        both = both.reshape(chunk * block, span).astype(BF16)
-        fown[some] = both.reshape(chunk, block, span)
-        both = jnp.dot(both, flip_lanes[...], preferred_element_type=F32).astype(BF16)
-        for k in range(chunk):
-            tile = both[k * block : (k + 1) * block]
-            tile = jnp.dot(unflip_rows[...], tile, preferred_element_type=F32)
-            fmsend[col_devices - 1 - i - k] = tile.astype(BF16)
-        some = pl.ds(col_devices - i - chunk, chunk)
-        fmcopy = pltpu.make_async_remote_copy(
+    def fmcopy(q, index, device):
+        some = pl.ds((chunks - 1 - q) * chunk, chunk)
+        return pltpu.make_async_remote_copy(
             src_ref=fmsend.at[some],
             dst_ref=fmrecv.at[some],
-            send_sem=sfm.at[i // chunk],
-            recv_sem=rfm.at[i // chunk],
-            device_id=partner,
+            send_sem=sfm.at[index],
+            recv_sem=rfm.at[q],
+            device_id=device,
             device_id_type=MESH,
         )
-        fmcopy.start()
-        fmcopies.append(fmcopy)
+
+    fmcopies = []
+    for j in range(chunks):
+        q = part(me_dp, j)
+        fcopy(q).wait_recv()
+        some = pl.ds(q * chunk, chunk)
+        both = fsend[some].astype(F32) + frecv[some].astype(F32)
+        both = both.astype(BF16)
+        fown[some] = both
+        back = both.reshape(chunk * keep, span)
+        back = jnp.dot(back, flip_lanes[...], preferred_element_type=F32).astype(BF16)
+        for i in range(chunk):
+            tile = back[i * keep : (i + 1) * keep]
+            tile = jnp.dot(unpick[side], tile, preferred_element_type=F32)
+            mirrored = col_devices - 1 - q * chunk - i
+            fmsend[mirrored] = tile[:keep].astype(BF16)
+            extra[pl.ds(2 * mirrored, 1)] = tile[keep : keep + 1]
+            extra[pl.ds(2 * mirrored + 1, 1)] = tile[keep + 1 : keep + 2]
+        if j < chunks // 2:
+            for w, device in enumerate([across, {"col": partner}]):
+                copy = fmcopy(q, 2 * j + w, device)
+                copy.start()
+                fmcopies.append(copy)
+    excopy.wait_recv()
+    both = fx[0].astype(F32) + fx[1].astype(F32)
+    fx[2] = (extra[...] + first * (both - extra[...])).astype(BF16)
+    fxcopy = send_one(fx.at[2], fx.at[3], 2, {"col": other})
 
     def put(index, src, dst):
         copy = pltpu.make_async_copy(src, dst, out_sem.at[index])
@@ -431,15 +523,19 @@
         grad_query[c] = (go[c].astype(F32) * conv).astype(BF16)
     puts.append(put(0, grad_query, grad_query_hbm))
 
+    fxcopy.wait_recv()
+    extra[...] = fx[3].astype(F32) * side.astype(F32)
+    top = lax.broadcasted_iota(jnp.int32, (8, span), 0) == 0
+    loads[17].wait()
     for k in reversed(range(col_devices)):
         if (k + 1) % chunk == 0:
-            fmcopies[(col_devices - 1 - k) // chunk].wait_recv()
-        mine, far = fown[k].astype(F32), fmrecv[k].astype(F32)
-        pieces = []
-        for p in range(2):
-            near, rest = mine[p * act : (p + 1) * act], far[p * keep // 2 : (p + 1) * keep // 2]
-            pieces += [near[: keep // 2], near[keep // 2 :] + rest[:8], rest[8:]]
-        flip[pl.ds(k, span, stride=col_devices), : 2 * keep] = jnp.concatenate(pieces, axis=0).T
+            fmcopy((col_devices - 1 - k) // chunk, 0, {"col": partner}).wait_recv()
+        tile = jnp.concatenate([fown[k], fmrecv[k]], axis=0)
+        tile = jnp.dot(merge[side], tile, preferred_element_type=F32)
+        re = jnp.where(top, tile[:8] + extra[2 * k : 2 * k + 1], tile[:8])
+        im = jnp.where(top, tile[keep : keep + 8] + extra[2 * k + 1 : 2 * k + 2], tile[keep : keep + 8])
+        tile = jnp.concatenate([re, tile[8:keep], im, tile[keep + 8 :]], axis=0)
+        flip[pl.ds(k, span, stride=col_devices), : 2 * keep] = tile.T
     for t in range(col_devices):
         lanes = slice(t * span, (t + 1) * span)
         tile = flip[lanes, : 2 * keep].T.astype(BF16)
@@ -460,7 +556,9 @@
 
     for a in range(2):
         wait_send(*row, a, send4, recv4, s4, r4)
-    for copy in fcopies + fmcopies + [mirror]:
+    for q in range(chunks):
+        fcopy(q).wait_send()
+    for copy in fmcopies + [mirror, mirror_far, excopy, fxcopy]:
         copy.wait_send()
     for copy in puts:
         copy.wait()
@@ -486,22 +584,20 @@
     rows_total = keep * col_devices
     half = rows_total // 2
     act = keep // 2 + 8
-    dims = (row_devices, col_devices, keep, span, rows_here)
+    dims = (row_devices, col_devices, keep, span)
     anywhere = pl.BlockSpec(memory_space=pl.ANY)
     token = jax.ShapeDtypeStruct((channels, rows_here, span), BF16)
     names = [
         "forward_high", "forward_low", "inverse_rows", "twist", "place",
-        "inner", "lane_high", "lane_low", "lane_inverse", "flip_lanes", "flip_rows",
-        "unflip_rows",
+        "inner", "lane_high", "lane_low", "lane_inverse", "flip_lanes", "pick",
+        "unpick", "merge", "half_twist",
     ]
     dma = pltpu.SemaphoreType.DMA
     tok = (2, row_devices, rows_here, span)
-    mid = (2, col_devices, 2 * act, span)
+    mid = (2, col_devices, keep, span)
     grad = (col_devices, 2 * act, span)
-    mirrored = (col_devices, keep, span)
     freq = jax.ShapeDtypeStruct((2, keep, cols_total), BF16)
-    chunks = (math.gcd(col_devices, 4),)
-    chunks = (col_devices // chunks[0],)
+    chunks = (4 if col_devices % 4 == 0 else 2,)
     outs = pl.pallas_call(
         functools.partial(kernel, dims),
         out_shape=[token, token, token, freq],
@@ -526,20 +622,24 @@
             pltpu.VMEM((col_devices, act, 2 * span), F32),
             pltpu.VMEM((2, col_devices, act, 2 * span), F32),
             pltpu.VMEM((2, keep // 2, cols_total), BF16),
+            pltpu.VMEM((2 * col_devices, span), F32),
+            pltpu.VMEM((2, 2 * col_devices, span), BF16),
             pltpu.VMEM((2, col_devices, act, span), F32),
-            pltpu.VMEM((2, col_devices, act, span), F32),
-            pltpu.VMEM(grad, BF16),
-            pltpu.VMEM(grad, BF16),
-            pltpu.VMEM(grad, BF16),
-            pltpu.VMEM(mirrored, BF16),
-            pltpu.VMEM(mirrored, BF16),
-            dma((17,)),
+            pltpu.VMEM((2, col_devices, keep // 2, span), F32),
+            pltpu.VMEM(mid[1:], BF16),
+            pltpu.VMEM(mid[1:], BF16),
+            pltpu.VMEM(mid[1:], BF16),
+            pltpu.VMEM(mid[1:], BF16),
+            pltpu.VMEM(mid[1:], BF16),
+            pltpu.VMEM((2 * col_devices, span), F32),
+            pltpu.VMEM((4, 2 * col_devices, span), BF16),
+            dma((19,)),
             dma((4,)),
             dma((4, 2)),
             dma((2,)), dma((2,)), dma((2,)), dma((2,)), dma((2,)), dma((2,)), dma((2,)), dma((2,)),
             dma(chunks), dma(chunks),
             dma(chunks), dma(chunks),
-            dma, dma,
+            dma((4,)), dma((4,)),
         ],
         compiler_params=pltpu.CompilerParams(
             collective_id=0, has_side_effects=True, vmem_limit_bytes=56 * 1024 * 1024

time: 61.8 us -> 60 us (0.971)
  Pallas kernels: 61 us -> 59.2 us
    pallas_call x1, Pallas kernels: 58.9 us -> 57.1 us  [shards(): pl.pallas_call(functools.partial(kernel, dims), out_shape=[token, token,...]
where the time goes in v4:
time: 60 us; the launch traced here: 59.9 us
  Pallas kernels  59.2 us (99%)
  between operations  0.64 us (1%)
    pallas_call x1, Pallas kernels, shards(): pl.pallas_call(functools.partial(kernel, dims), out_shape=[token, token,...  57.1 us
    pallas_call x1, Pallas kernels, shards(): pl.pallas_call(hand_over, out_shape=[jax.ShapeDtypeStruct(out.shape, out....  2.11 us

profile of v4, /device:TPU:1, one launch (start us, length us, event | category | flops | bytes accessed | tf_op | source)
XLA Modules:
  0.0 59.9 jit_solution(14829007923080198597)
XLA Ops:
  0.6 57.1 %hyena_backward.1 = (bf16[16,32,128]{2,1,0:T(8,128)(2,1)}, bf16[16,32,128]{2,1,0:T(8,128)(2,1)}, bf16[16,32,128]{2,1,0:T(8,128)(2,1)}, bf16[2,64,2048]{2,1,0:T(8,128)(2,1)}) custom-call(bf16[16,32,128]{2,1,0:T(8,128)(2,1)} %bitcast.12, bf16[16,32,128]{2,1,0:T(8,128)(2,1)} %bitcast.13, bf16[16,32,128]{2,1,0:T(8,128)(2,1)} %bitcast.14, ...), custom_call_target="tpu_custom_call" | custom-call | tf_op jit(solution)/shard_map/hyena_backward/pallas_call | solution.py:601
  57.7 2.1 %hand_over.1 = (bf16[16,32,128]{2,1,0:T(8,128)(2,1)}, bf16[16,32,128]{2,1,0:T(8,128)(2,1)}, bf16[16,32,128]{2,1,0:T(8,128)(2,1)}, bf16[2,64,2048]{2,1,0:T(8,128)(2,1)}) custom-call(bf16[16,32,128]{2,1,0:T(8,128)(2,1)} %get-tuple-element.12.refs_0_, bf16[16,32,128]{2,1,0:T(8,128)(2,1)} %get-tuple-element.13.refs_1_, ...), custom_call_target="tpu_custom_call" | custom-call | tf_op jit(solution)/shard_map/hand_over/pallas_call | solution.py:652

commit v5 on v4

--- a/solution.py
+++ b/solution.py
@@ -138,8 +138,12 @@
     return out
 
 
-def ring_order(size):
-    return sorted(range(1, size), key=lambda s: -min(s, size - s))
+def far_first(size, send):
+    def body(i, carry):
+        send(size // 2 + lax.div(i + 1, 2) * (1 - 2 * lax.rem(i, 2)))
+        return carry
+
+    lax.fori_loop(0, size - 1, body, 0)
 
 
 def kernel(
@@ -226,8 +230,10 @@
         prod[a] = (left[...].astype(F32) * right[...].astype(F32)).astype(BF16)
         if a == 0:
             pl.semaphore_wait(barrier, row_devices + col_devices)
-        for s in ring_order(row_devices):
-            exchange(*row, a, prod, recv1, s1, r1, lax.rem(me_row + s, row_devices)).start()
+        far_first(
+            row_devices,
+            lambda s: exchange(*row, a, prod, recv1, s1, r1, lax.rem(me_row + s, row_devices)).start(),
+        )
         own(me_row, a, prod, recv1, 0).start()
 
     loads[4].wait()
@@ -258,8 +264,9 @@
 
     loads[5].wait()
     loads[6].wait()
-    for c in range(col_devices):
-        rows = pl.ds(c * wire, wire)
+    @pl.loop(0, col_devices)
+    def _(c):
+        rows = pl.ds(pl.multiple_of(c * wire, wire), wire)
         lane = lax.broadcasted_iota(jnp.int32, (wire, 128), 1) == me_col
         pr = jnp.sum(jnp.where(lane, place[0, rows], 0.0), axis=1, keepdims=True)
         pi = jnp.sum(jnp.where(lane, place[1, rows], 0.0), axis=1, keepdims=True)
@@ -422,8 +429,10 @@
         w = jnp.concatenate(parts, axis=0).astype(BF16)
         total = jnp.dot(inv_rows[...], w, preferred_element_type=F32)
         send4[a] = total.astype(BF16).reshape(row_devices, half // row_devices, span)
-        for s in ring_order(row_devices):
-            exchange(*row, a, send4, recv4, s4, r4, lax.rem(me_row + s, row_devices)).start()
+        far_first(
+            row_devices,
+            lambda s: exchange(*row, a, send4, recv4, s4, r4, lax.rem(me_row + s, row_devices)).start(),
+        )
         own(me_row, a, send4, recv4, 3).start()
 
     loads[7].wait()
@@ -518,9 +527,11 @@
 
     puts = []
     wait_recv(*row, 0, send4, recv4, s4, r4, 3)
-    for c in range(row_devices):
+    @pl.loop(0, row_devices)
+    def _(c):
         conv = recv4[0, c].astype(F32) + gain[c] * prod[0, c].astype(F32)
         grad_query[c] = (go[c].astype(F32) * conv).astype(BF16)
+
     puts.append(put(0, grad_query, grad_query_hbm))
 
     fxcopy.wait_recv()
@@ -547,10 +558,12 @@
         wait_send(*col, a, send2, recv2, s2, r2)
         wait_send(*col, a, send3, recv3, s3, r3)
     wait_recv(*row, 1, send4, recv4, s4, r4, 3)
-    for c in range(row_devices):
+    @pl.loop(0, row_devices)
+    def _(c):
         mixed_grad = recv4[1, c].astype(F32) + gain[c] * prod[1, c].astype(F32)
         grad_key[c] = (mixed_grad * vi[c].astype(F32)).astype(BF16)
         grad_value[c] = (mixed_grad * gk[c].astype(F32)).astype(BF16)
+
     puts.append(put(2, grad_key, grad_key_hbm))
     puts.append(put(3, grad_value, grad_value_hbm))
 

time: 60 us -> 60 us (level)
  no operation moved by 1% of the time
where the time goes in v5:
time: 60 us; the launch traced here: 59.9 us
  Pallas kernels  59.2 us (99%)
  between operations  0.64 us (1%)
    pallas_call x1, Pallas kernels, shards(): pl.pallas_call(functools.partial(kernel, dims), out_shape=[token, token,...  57.1 us
    pallas_call x1, Pallas kernels, shards(): pl.pallas_call(hand_over, out_shape=[jax.ShapeDtypeStruct(out.shape, out....  2.11 us

profile of v5, /device:TPU:1, one launch (start us, length us, event | category | flops | bytes accessed | tf_op | source)
XLA Modules:
  0.0 59.9 jit_solution(1551204146824595752)
XLA Ops:
  0.6 57.1 %hyena_backward.1 = (bf16[16,32,128]{2,1,0:T(8,128)(2,1)}, bf16[16,32,128]{2,1,0:T(8,128)(2,1)}, bf16[16,32,128]{2,1,0:T(8,128)(2,1)}, bf16[2,64,2048]{2,1,0:T(8,128)(2,1)}) custom-call(bf16[16,32,128]{2,1,0:T(8,128)(2,1)} %bitcast.12, bf16[16,32,128]{2,1,0:T(8,128)(2,1)} %bitcast.13, bf16[16,32,128]{2,1,0:T(8,128)(2,1)} %bitcast.14, ...), custom_call_target="tpu_custom_call" | custom-call | tf_op jit(solution)/shard_map/hyena_backward/pallas_call | solution.py:614
  57.8 2.1 %hand_over.1 = (bf16[16,32,128]{2,1,0:T(8,128)(2,1)}, bf16[16,32,128]{2,1,0:T(8,128)(2,1)}, bf16[16,32,128]{2,1,0:T(8,128)(2,1)}, bf16[2,64,2048]{2,1,0:T(8,128)(2,1)}) custom-call(bf16[16,32,128]{2,1,0:T(8,128)(2,1)} %get-tuple-element.12.refs_0_, bf16[16,32,128]{2,1,0:T(8,128)(2,1)} %get-tuple-element.13.refs_1_, ...), custom_call_target="tpu_custom_call" | custom-call | tf_op jit(solution)/shard_map/hand_over/pallas_call | solution.py:665
